TPU v7x, 32 devices: a whole 2x2x4 slice. The times are simulated.
32 devices in a mesh: grp: 2 (over y), gx: 4 (over z), gy: 2 (over core), shot: 2 (over x).
Axes of the slice: x: 2, y: 2, z: 4, core: 2. Of those that a mesh axis runs over, the one named last changes fastest.
Arguments:
- courant_sq: float32 [128, 64, 256], P('grp', 'gx', 'gy'), parts along dimension 0, may hold values from 0.02 to 0.2
- pressure_start: float32 [4, 64, 64, 256], P(('grp', 'shot'), None, 'gx', 'gy'), parts along dimension 0, may hold values from -6 to 6
- previous_start: float32 [4, 64, 64, 256], P(('grp', 'shot'), None, 'gx', 'gy'), parts along dimension 0, may hold values from -6 to 6
- wavelets: float32 [32, 20], P(('grp', 'shot')), parts along dimension 0, may hold values from -6 to 6
- traces: float32 [32, 20, 64, 256], P(('grp', 'shot'), None, 'gx', 'gy'), parts along dimension 0, may hold values from -1.5 to 1.5
- code_bits: int32 [32], P(('grp', 'shot')), parts along dimension 0, may hold values from 0 to 1
- assign: int32 [32], P(('grp', 'shot')), parts along dimension 0, may hold values from 0 to 1, as said below
- pos_x: int32 [32], P(('grp', 'shot')), parts along dimension 0, may hold values from 0 to 63
- pos_y: int32 [32], P(('grp', 'shot')), parts along dimension 0, may hold values from 0 to 255
Outputs:
- pressure: float32 [4, 64, 64, 256], P(('grp', 'shot'), None, 'gx', 'gy'), parts along dimension 0
- misfit: float32 [4, 20, 64, 256], P(('grp', 'shot'), None, 'gx', 'gy'), parts along dimension 0
There are 2 independent parts, one for each index of `grp`. A program takes and returns all parts, laid end to end along the dimension named above; each array names one. Nothing has to cross between parts.
Inputs may be any that keep to these rules, and one draw needn't show every extreme that they name: `assign`: each supershot is the supershot of exactly 8 shots.
All inputs are finite; a program needn't handle non-finite values.
Results may differ from a plain program's by a relative error of at most 0.00027.
Values sent between devices are 32-bit elements; how exact they have to be, the bound alone decides.
A program may use at most 64 MiB of HBM per device.

v0:
```python
import jax
import jax.numpy as jnp
from jax import lax
from jax.sharding import PartitionSpec as P

SUP_DEV = 1


coeffs = (-205.0 / 72.0, 8.0 / 5.0, -1.0 / 5.0, 8.0 / 315.0, -1.0 / 560.0)
source_layer = 2
record_layer = 6


def with_halo(block, sides, width):
    for axis, dim in sides:
        count = lax.axis_size(axis)
        forward = [(i, i + 1) for i in range(count - 1)]
        backward = [(target, source) for source, target in forward]
        low = lax.ppermute(
            lax.slice_in_dim(block, block.shape[dim] - width, None, axis=dim), axis, forward
        )
        high = lax.ppermute(lax.slice_in_dim(block, 0, width, axis=dim), axis, backward)
        block = jnp.concatenate([low, block, high], axis=dim)
    return block


def laplace_inner(wide):
    depth = wide.shape[1]
    out_x = wide.shape[2] - 8
    out_y = wide.shape[3] - 8
    padded = jnp.pad(wide, ((0, 0), (4, 4), (0, 0), (0, 0)))

    def piece(dz, dx, dy):
        return padded[:, 4 + dz : 4 + dz + depth, 4 + dx : 4 + dx + out_x, 4 + dy : 4 + dy + out_y]

    total = 3.0 * coeffs[0] * piece(0, 0, 0)
    for j in range(1, 5):
        total = total + coeffs[j] * (piece(j, 0, 0) + piece(-j, 0, 0))
        total = total + coeffs[j] * (piece(0, j, 0) + piece(0, -j, 0))
        total = total + coeffs[j] * (piece(0, 0, j) + piece(0, 0, -j))
    return total


def advance(wide, previous, speed, source_now):
    center = wide[:, :, 4:-4, 4:-4]
    nxt = 2.0 * center - previous + speed[None] * laplace_inner(wide)
    return nxt.at[:, source_layer].add(source_now)


def make_encode(code_bits, assign, nsup):
    signs = (2 * code_bits - 1).astype(jnp.float32)
    return signs[:, None] * (assign[:, None] == jnp.arange(nsup, dtype=jnp.int32)[None, :]).astype(
        jnp.float32
    )


def make_place(pos_x, pos_y, width_x, width_y):
    local_x = pos_x - lax.axis_index("gx") * width_x
    local_y = pos_y - lax.axis_index("gy") * width_y
    onex = (local_x[:, None] == jnp.arange(width_x, dtype=jnp.int32)[None, :]).astype(jnp.float32)
    oney = (local_y[:, None] == jnp.arange(width_y, dtype=jnp.int32)[None, :]).astype(jnp.float32)
    return onex[:, :, None] * oney[:, None, :]


def on_device(
    courant_sq, pressure_start, previous_start, wavelets, traces, code_bits, assign, pos_x, pos_y
):
    width_x = courant_sq.shape[1]
    width_y = courant_sq.shape[2]
    steps = wavelets.shape[1]
    nsup = SUP_DEV * lax.axis_size("shot")
    encode = make_encode(code_bits, assign, nsup)
    observed_part = jnp.einsum("sk,stxy->ktxy", encode, traces, precision=lax.Precision.HIGHEST)
    place = make_place(pos_x, pos_y, width_x, width_y)
    weighted = encode[:, :, None] * wavelets[:, None, :]
    sources_part = jnp.einsum("skt,sxy->ktxy", weighted, place, precision=lax.Precision.HIGHEST)
    mine = lax.psum_scatter(
        jnp.stack([sources_part, observed_part], axis=1), "shot", scatter_dimension=0, tiled=True
    )
    sources = mine[:, 0]
    observed = mine[:, 1]
    pressure = pressure_start
    previous = previous_start
    misfit = jnp.zeros((SUP_DEV, steps, width_x, width_y), jnp.float32)

    def one_step(index, carry):
        current, older, record = carry
        wide = with_halo(current, (("gx", 2), ("gy", 3)), 4)
        source_now = lax.dynamic_index_in_dim(sources, index, 1, keepdims=False)
        nxt = advance(wide, older, courant_sq, source_now)
        row = nxt[:, record_layer] - lax.dynamic_index_in_dim(observed, index, 1, keepdims=False)
        record = lax.dynamic_update_index_in_dim(record, row, index, 1)
        return (nxt, current, record)

    pressure, previous, misfit = lax.fori_loop(0, steps, one_step, (pressure, previous, misfit))
    return (pressure, misfit)


def solution(mesh):
    return jax.shard_map(
        on_device,
        mesh=mesh,
        in_specs=(
            P("grp", "gx", "gy"),
            P(("grp", "shot"), None, "gx", "gy"),
            P(("grp", "shot"), None, "gx", "gy"),
            P(("grp", "shot"), None),
            P(("grp", "shot"), None, "gx", "gy"),
            P(("grp", "shot")),
            P(("grp", "shot")),
            P(("grp", "shot")),
            P(("grp", "shot")),
        ),
        out_specs=(P(("grp", "shot"), None, "gx", "gy"), P(("grp", "shot"), None, "gx", "gy")),
        check_vma=False,
    )
```

profile of v0, /device:TPU:1, one launch (start us, length us, event | category | flops | bytes accessed | tf_op | source)
XLA Modules:
  0.0 880.4 jit_solution(16974322734794268449)
XLA Ops:
  16.8 14.7 %reduce-scatter.2.cloned.1.call-done = f32[1,2,20,16,128]{4,3,2,1,0:T(8,128)} async-done(((f32[2,2,20,16,128]{4,3,2,1,0:T(8,128)}), f32[1,2,20,16,128]{4,3,2,1,0:T(8,128)}) %reduce-scatter.2.cloned.1.call-update) | async-done | bytes 327696 | tf_op jit(solution)/shard_map/reduce_scatter | solution.py:77
  33.2 839.0 %while.20 = (s32[]{:T(128)}, f32[1,64,16,128]{1,2,3,0:T(8,128)S(1)}, f32[1,64,16,128]{1,2,3,0:T(8,128)}, f32[1,20,16,128]{3,2,1,0:T(8,128)}, f32[64,16,128]{0,1,...) while((s32[]{:T(128)}, ...), condition=%wide.region_2.3_spmd, body=%wide.region_1.2_spmd.sunk | while | flops 9963522 | bytes 28694948 | solution.py:95
  54.0 4.8 fusion.51
  60.7 10.7 %scatter-add.6 = f32[1,64,16,128]{1,2,3,0:T(8,128)S(1)} dynamic-update-slice(f32[1,64,16,128]{1,2,3,0:T(8,128)S(1)} %fusion.51, f32[1,1,16,128]{1,2,3,0:T(8,128)S(1)} %slice_add_fusion.10, s32[]{:T(128)} %constant.180.clone.1..sunk, s32[]{:T(128)} %constant.178.clone.1..sunk, s32[]{:T(128)} %constant.180.clone.1..sunk, s32[]{:T(128)} %constant.180.clone.1..sunk) | dynamic-update-slice | bytes 16388 | tf_op jit(solution)/shard_map/while/body/eval_jaxpr/scatter-add | solution.py:47
  96.9 4.8 fusion.51
  103.7 10.7 %scatter-add.6 = f32[1,64,16,128]{1,2,3,0:T(8,128)S(1)} dynamic-update-slice(f32[1,64,16,128]{1,2,3,0:T(8,128)S(1)} %fusion.51, f32[1,1,16,128]{1,2,3,0:T(8,128)S(1)} %slice_add_fusion.10, s32[]{:T(128)} %constant.180.clone.1..sunk, s32[]{:T(128)} %constant.178.clone.1..sunk, s32[]{:T(128)} %constant.180.clone.1..sunk, s32[]{:T(128)} %constant.180.clone.1..sunk) | dynamic-update-slice | bytes 16388 | tf_op jit(solution)/shard_map/while/body/eval_jaxpr/scatter-add | solution.py:47
  127.9 3.8 collective-permute-done.1
  139.9 4.8 fusion.51
  146.6 10.7 %scatter-add.6 = f32[1,64,16,128]{1,2,3,0:T(8,128)S(1)} dynamic-update-slice(f32[1,64,16,128]{1,2,3,0:T(8,128)S(1)} %fusion.51, f32[1,1,16,128]{1,2,3,0:T(8,128)S(1)} %slice_add_fusion.10, s32[]{:T(128)} %constant.180.clone.1..sunk, s32[]{:T(128)} %constant.178.clone.1..sunk, s32[]{:T(128)} %constant.180.clone.1..sunk, s32[]{:T(128)} %constant.180.clone.1..sunk) | dynamic-update-slice | bytes 16388 | tf_op jit(solution)/shard_map/while/body/eval_jaxpr/scatter-add | solution.py:47
  181.7 4.8 fusion.51
  188.4 10.7 %scatter-add.6 = f32[1,64,16,128]{1,2,3,0:T(8,128)S(1)} dynamic-update-slice(f32[1,64,16,128]{1,2,3,0:T(8,128)S(1)} %fusion.51, f32[1,1,16,128]{1,2,3,0:T(8,128)S(1)} %slice_add_fusion.10, s32[]{:T(128)} %constant.180.clone.1..sunk, s32[]{:T(128)} %constant.178.clone.1..sunk, s32[]{:T(128)} %constant.180.clone.1..sunk, s32[]{:T(128)} %constant.180.clone.1..sunk) | dynamic-update-slice | bytes 16388 | tf_op jit(solution)/shard_map/while/body/eval_jaxpr/scatter-add | solution.py:47
  223.5 4.8 fusion.51
  230.2 10.7 %scatter-add.6 = f32[1,64,16,128]{1,2,3,0:T(8,128)S(1)} dynamic-update-slice(f32[1,64,16,128]{1,2,3,0:T(8,128)S(1)} %fusion.51, f32[1,1,16,128]{1,2,3,0:T(8,128)S(1)} %slice_add_fusion.10, s32[]{:T(128)} %constant.180.clone.1..sunk, s32[]{:T(128)} %constant.178.clone.1..sunk, s32[]{:T(128)} %constant.180.clone.1..sunk, s32[]{:T(128)} %constant.180.clone.1..sunk) | dynamic-update-slice | bytes 16388 | tf_op jit(solution)/shard_map/while/body/eval_jaxpr/scatter-add | solution.py:47
  253.2 3.8 collective-permute-done.1
  265.2 4.8 fusion.51
  271.9 10.7 %scatter-add.6 = f32[1,64,16,128]{1,2,3,0:T(8,128)S(1)} dynamic-update-slice(f32[1,64,16,128]{1,2,3,0:T(8,128)S(1)} %fusion.51, f32[1,1,16,128]{1,2,3,0:T(8,128)S(1)} %slice_add_fusion.10, s32[]{:T(128)} %constant.180.clone.1..sunk, s32[]{:T(128)} %constant.178.clone.1..sunk, s32[]{:T(128)} %constant.180.clone.1..sunk, s32[]{:T(128)} %constant.180.clone.1..sunk) | dynamic-update-slice | bytes 16388 | tf_op jit(solution)/shard_map/while/body/eval_jaxpr/scatter-add | solution.py:47
  307.0 4.8 fusion.51
  313.7 10.7 %scatter-add.6 = f32[1,64,16,128]{1,2,3,0:T(8,128)S(1)} dynamic-update-slice(f32[1,64,16,128]{1,2,3,0:T(8,128)S(1)} %fusion.51, f32[1,1,16,128]{1,2,3,0:T(8,128)S(1)} %slice_add_fusion.10, s32[]{:T(128)} %constant.180.clone.1..sunk, s32[]{:T(128)} %constant.178.clone.1..sunk, s32[]{:T(128)} %constant.180.clone.1..sunk, s32[]{:T(128)} %constant.180.clone.1..sunk) | dynamic-update-slice | bytes 16388 | tf_op jit(solution)/shard_map/while/body/eval_jaxpr/scatter-add | solution.py:47
  348.8 4.8 fusion.51
  355.5 10.7 %scatter-add.6 = f32[1,64,16,128]{1,2,3,0:T(8,128)S(1)} dynamic-update-slice(f32[1,64,16,128]{1,2,3,0:T(8,128)S(1)} %fusion.51, f32[1,1,16,128]{1,2,3,0:T(8,128)S(1)} %slice_add_fusion.10, s32[]{:T(128)} %constant.180.clone.1..sunk, s32[]{:T(128)} %constant.178.clone.1..sunk, s32[]{:T(128)} %constant.180.clone.1..sunk, s32[]{:T(128)} %constant.180.clone.1..sunk) | dynamic-update-slice | bytes 16388 | tf_op jit(solution)/shard_map/while/body/eval_jaxpr/scatter-add | solution.py:47
  378.5 3.8 collective-permute-done.1
  390.5 4.8 fusion.51
  397.2 10.7 %scatter-add.6 = f32[1,64,16,128]{1,2,3,0:T(8,128)S(1)} dynamic-update-slice(f32[1,64,16,128]{1,2,3,0:T(8,128)S(1)} %fusion.51, f32[1,1,16,128]{1,2,3,0:T(8,128)S(1)} %slice_add_fusion.10, s32[]{:T(128)} %constant.180.clone.1..sunk, s32[]{:T(128)} %constant.178.clone.1..sunk, s32[]{:T(128)} %constant.180.clone.1..sunk, s32[]{:T(128)} %constant.180.clone.1..sunk) | dynamic-update-slice | bytes 16388 | tf_op jit(solution)/shard_map/while/body/eval_jaxpr/scatter-add | solution.py:47
  432.3 4.8 fusion.51
  439.0 10.7 %scatter-add.6 = f32[1,64,16,128]{1,2,3,0:T(8,128)S(1)} dynamic-update-slice(f32[1,64,16,128]{1,2,3,0:T(8,128)S(1)} %fusion.51, f32[1,1,16,128]{1,2,3,0:T(8,128)S(1)} %slice_add_fusion.10, s32[]{:T(128)} %constant.180.clone.1..sunk, s32[]{:T(128)} %constant.178.clone.1..sunk, s32[]{:T(128)} %constant.180.clone.1..sunk, s32[]{:T(128)} %constant.180.clone.1..sunk) | dynamic-update-slice | bytes 16388 | tf_op jit(solution)/shard_map/while/body/eval_jaxpr/scatter-add | solution.py:47
  462.0 3.8 collective-permute-done.1
  474.1 4.8 fusion.51
  480.8 10.7 %scatter-add.6 = f32[1,64,16,128]{1,2,3,0:T(8,128)S(1)} dynamic-update-slice(f32[1,64,16,128]{1,2,3,0:T(8,128)S(1)} %fusion.51, f32[1,1,16,128]{1,2,3,0:T(8,128)S(1)} %slice_add_fusion.10, s32[]{:T(128)} %constant.180.clone.1..sunk, s32[]{:T(128)} %constant.178.clone.1..sunk, s32[]{:T(128)} %constant.180.clone.1..sunk, s32[]{:T(128)} %constant.180.clone.1..sunk) | dynamic-update-slice | bytes 16388 | tf_op jit(solution)/shard_map/while/body/eval_jaxpr/scatter-add | solution.py:47
  515.9 4.8 fusion.51
  522.6 10.7 %scatter-add.6 = f32[1,64,16,128]{1,2,3,0:T(8,128)S(1)} dynamic-update-slice(f32[1,64,16,128]{1,2,3,0:T(8,128)S(1)} %fusion.51, f32[1,1,16,128]{1,2,3,0:T(8,128)S(1)} %slice_add_fusion.10, s32[]{:T(128)} %constant.180.clone.1..sunk, s32[]{:T(128)} %constant.178.clone.1..sunk, s32[]{:T(128)} %constant.180.clone.1..sunk, s32[]{:T(128)} %constant.180.clone.1..sunk) | dynamic-update-slice | bytes 16388 | tf_op jit(solution)/shard_map/while/body/eval_jaxpr/scatter-add | solution.py:47
  557.6 4.8 fusion.51
  564.3 10.7 %scatter-add.6 = f32[1,64,16,128]{1,2,3,0:T(8,128)S(1)} dynamic-update-slice(f32[1,64,16,128]{1,2,3,0:T(8,128)S(1)} %fusion.51, f32[1,1,16,128]{1,2,3,0:T(8,128)S(1)} %slice_add_fusion.10, s32[]{:T(128)} %constant.180.clone.1..sunk, s32[]{:T(128)} %constant.178.clone.1..sunk, s32[]{:T(128)} %constant.180.clone.1..sunk, s32[]{:T(128)} %constant.180.clone.1..sunk) | dynamic-update-slice | bytes 16388 | tf_op jit(solution)/shard_map/while/body/eval_jaxpr/scatter-add | solution.py:47
  587.3 3.8 collective-permute-done.1
  599.4 4.8 fusion.51
  606.1 10.7 %scatter-add.6 = f32[1,64,16,128]{1,2,3,0:T(8,128)S(1)} dynamic-update-slice(f32[1,64,16,128]{1,2,3,0:T(8,128)S(1)} %fusion.51, f32[1,1,16,128]{1,2,3,0:T(8,128)S(1)} %slice_add_fusion.10, s32[]{:T(128)} %constant.180.clone.1..sunk, s32[]{:T(128)} %constant.178.clone.1..sunk, s32[]{:T(128)} %constant.180.clone.1..sunk, s32[]{:T(128)} %constant.180.clone.1..sunk) | dynamic-update-slice | bytes 16388 | tf_op jit(solution)/shard_map/while/body/eval_jaxpr/scatter-add | solution.py:47
  641.2 4.8 fusion.51
  647.9 10.7 %scatter-add.6 = f32[1,64,16,128]{1,2,3,0:T(8,128)S(1)} dynamic-update-slice(f32[1,64,16,128]{1,2,3,0:T(8,128)S(1)} %fusion.51, f32[1,1,16,128]{1,2,3,0:T(8,128)S(1)} %slice_add_fusion.10, s32[]{:T(128)} %constant.180.clone.1..sunk, s32[]{:T(128)} %constant.178.clone.1..sunk, s32[]{:T(128)} %constant.180.clone.1..sunk, s32[]{:T(128)} %constant.180.clone.1..sunk) | dynamic-update-slice | bytes 16388 | tf_op jit(solution)/shard_map/while/body/eval_jaxpr/scatter-add | solution.py:47
  682.9 4.8 fusion.51
  689.6 10.7 %scatter-add.6 = f32[1,64,16,128]{1,2,3,0:T(8,128)S(1)} dynamic-update-slice(f32[1,64,16,128]{1,2,3,0:T(8,128)S(1)} %fusion.51, f32[1,1,16,128]{1,2,3,0:T(8,128)S(1)} %slice_add_fusion.10, s32[]{:T(128)} %constant.180.clone.1..sunk, s32[]{:T(128)} %constant.178.clone.1..sunk, s32[]{:T(128)} %constant.180.clone.1..sunk, s32[]{:T(128)} %constant.180.clone.1..sunk) | dynamic-update-slice | bytes 16388 | tf_op jit(solution)/shard_map/while/body/eval_jaxpr/scatter-add | solution.py:47
  712.7 3.8 collective-permute-done.1
  724.7 4.8 fusion.51
  731.4 10.7 %scatter-add.6 = f32[1,64,16,128]{1,2,3,0:T(8,128)S(1)} dynamic-update-slice(f32[1,64,16,128]{1,2,3,0:T(8,128)S(1)} %fusion.51, f32[1,1,16,128]{1,2,3,0:T(8,128)S(1)} %slice_add_fusion.10, s32[]{:T(128)} %constant.180.clone.1..sunk, s32[]{:T(128)} %constant.178.clone.1..sunk, s32[]{:T(128)} %constant.180.clone.1..sunk, s32[]{:T(128)} %constant.180.clone.1..sunk) | dynamic-update-slice | bytes 16388 | tf_op jit(solution)/shard_map/while/body/eval_jaxpr/scatter-add | solution.py:47
  766.5 4.8 fusion.51
  773.2 10.7 %scatter-add.6 = f32[1,64,16,128]{1,2,3,0:T(8,128)S(1)} dynamic-update-slice(f32[1,64,16,128]{1,2,3,0:T(8,128)S(1)} %fusion.51, f32[1,1,16,128]{1,2,3,0:T(8,128)S(1)} %slice_add_fusion.10, s32[]{:T(128)} %constant.180.clone.1..sunk, s32[]{:T(128)} %constant.178.clone.1..sunk, s32[]{:T(128)} %constant.180.clone.1..sunk, s32[]{:T(128)} %constant.180.clone.1..sunk) | dynamic-update-slice | bytes 16388 | tf_op jit(solution)/shard_map/while/body/eval_jaxpr/scatter-add | solution.py:47
  808.3 4.8 fusion.51
  815.0 10.7 %scatter-add.6 = f32[1,64,16,128]{1,2,3,0:T(8,128)S(1)} dynamic-update-slice(f32[1,64,16,128]{1,2,3,0:T(8,128)S(1)} %fusion.51, f32[1,1,16,128]{1,2,3,0:T(8,128)S(1)} %slice_add_fusion.10, s32[]{:T(128)} %constant.180.clone.1..sunk, s32[]{:T(128)} %constant.178.clone.1..sunk, s32[]{:T(128)} %constant.180.clone.1..sunk, s32[]{:T(128)} %constant.180.clone.1..sunk) | dynamic-update-slice | bytes 16388 | tf_op jit(solution)/shard_map/while/body/eval_jaxpr/scatter-add | solution.py:47
  850.0 4.8 fusion.51
  856.7 10.7 %scatter-add.6 = f32[1,64,16,128]{1,2,3,0:T(8,128)S(1)} dynamic-update-slice(f32[1,64,16,128]{1,2,3,0:T(8,128)S(1)} %fusion.51, f32[1,1,16,128]{1,2,3,0:T(8,128)S(1)} %slice_add_fusion.10, s32[]{:T(128)} %constant.180.clone.1..sunk, s32[]{:T(128)} %constant.178.clone.1..sunk, s32[]{:T(128)} %constant.180.clone.1..sunk, s32[]{:T(128)} %constant.180.clone.1..sunk) | dynamic-update-slice | bytes 16388 | tf_op jit(solution)/shard_map/while/body/eval_jaxpr/scatter-add | solution.py:47
  (687 shorter events, 517.1 us)
Async XLA Ops:
  7.2 24.2 %reduce-scatter.2.cloned.1.call-start = ((), (), s32[]{:S(2)}) async-start(), calls=%async_computation.1 | async-start | bytes 983040 | tf_op jit(solution)/shard_map/reduce_scatter | solution.py:77
  33.3 8.1 collective-permute-start
  36.4 8.8 collective-permute-start.1
  45.2 5.2 collective-permute-start.2
  76.2 8.7 collective-permute-start
  79.4 9.3 %collective-permute-start.1 = (f32[1,64,4,128]{1,2,3,0:T(4,128)S(1)}, f32[1,64,4,128]{1,2,3,0:T(4,128)S(1)}, u32[]{:S(2)}, u32[]{:S(2)}) collective-permute-start(f32[1,64,4,128]{1,2,3,0:T(4,128)S(1)} %get-tuple-element.315), channel_id=1, source_target_pairs={{4,0},{8,4},{12,8},{5,1},{9,5},{13,9},{6,2},{10,6},{14,10},{7,3},{... | collective-permute-start | bytes 393224 | tf_op jit(solution)/shard_map/while/body/eval_jaxpr/ppermute | solution.py:22
  88.7 4.6 collective-permute-start.2
  119.2 8.7 collective-permute-start
  122.3 9.3 %collective-permute-start.1 = (f32[1,64,4,128]{1,2,3,0:T(4,128)S(1)}, f32[1,64,4,128]{1,2,3,0:T(4,128)S(1)}, u32[]{:S(2)}, u32[]{:S(2)}) collective-permute-start(f32[1,64,4,128]{1,2,3,0:T(4,128)S(1)} %get-tuple-element.315), channel_id=1, source_target_pairs={{4,0},{8,4},{12,8},{5,1},{9,5},{13,9},{6,2},{10,6},{14,10},{7,3},{... | collective-permute-start | bytes 393224 | tf_op jit(solution)/shard_map/while/body/eval_jaxpr/ppermute | solution.py:22
  162.2 7.5 collective-permute-start
  164.1 9.3 %collective-permute-start.1 = (f32[1,64,4,128]{1,2,3,0:T(4,128)S(1)}, f32[1,64,4,128]{1,2,3,0:T(4,128)S(1)}, u32[]{:S(2)}, u32[]{:S(2)}) collective-permute-start(f32[1,64,4,128]{1,2,3,0:T(4,128)S(1)} %get-tuple-element.315), channel_id=1, source_target_pairs={{4,0},{8,4},{12,8},{5,1},{9,5},{13,9},{6,2},{10,6},{14,10},{7,3},{... | collective-permute-start | bytes 393224 | tf_op jit(solution)/shard_map/while/body/eval_jaxpr/ppermute | solution.py:22
  204.0 7.5 collective-permute-start
  205.9 9.3 %collective-permute-start.1 = (f32[1,64,4,128]{1,2,3,0:T(4,128)S(1)}, f32[1,64,4,128]{1,2,3,0:T(4,128)S(1)}, u32[]{:S(2)}, u32[]{:S(2)}) collective-permute-start(f32[1,64,4,128]{1,2,3,0:T(4,128)S(1)} %get-tuple-element.315), channel_id=1, source_target_pairs={{4,0},{8,4},{12,8},{5,1},{9,5},{13,9},{6,2},{10,6},{14,10},{7,3},{... | collective-permute-start | bytes 393224 | tf_op jit(solution)/shard_map/while/body/eval_jaxpr/ppermute | solution.py:22
  245.7 7.5 collective-permute-start
  247.7 9.3 %collective-permute-start.1 = (f32[1,64,4,128]{1,2,3,0:T(4,128)S(1)}, f32[1,64,4,128]{1,2,3,0:T(4,128)S(1)}, u32[]{:S(2)}, u32[]{:S(2)}) collective-permute-start(f32[1,64,4,128]{1,2,3,0:T(4,128)S(1)} %get-tuple-element.315), channel_id=1, source_target_pairs={{4,0},{8,4},{12,8},{5,1},{9,5},{13,9},{6,2},{10,6},{14,10},{7,3},{... | collective-permute-start | bytes 393224 | tf_op jit(solution)/shard_map/while/body/eval_jaxpr/ppermute | solution.py:22
  257.0 4.6 collective-permute-start.2
  287.5 7.5 collective-permute-start
  289.4 9.3 %collective-permute-start.1 = (f32[1,64,4,128]{1,2,3,0:T(4,128)S(1)}, f32[1,64,4,128]{1,2,3,0:T(4,128)S(1)}, u32[]{:S(2)}, u32[]{:S(2)}) collective-permute-start(f32[1,64,4,128]{1,2,3,0:T(4,128)S(1)} %get-tuple-element.315), channel_id=1, source_target_pairs={{4,0},{8,4},{12,8},{5,1},{9,5},{13,9},{6,2},{10,6},{14,10},{7,3},{... | collective-permute-start | bytes 393224 | tf_op jit(solution)/shard_map/while/body/eval_jaxpr/ppermute | solution.py:22
  329.3 7.5 collective-permute-start
  331.2 9.3 %collective-permute-start.1 = (f32[1,64,4,128]{1,2,3,0:T(4,128)S(1)}, f32[1,64,4,128]{1,2,3,0:T(4,128)S(1)}, u32[]{:S(2)}, u32[]{:S(2)}) collective-permute-start(f32[1,64,4,128]{1,2,3,0:T(4,128)S(1)} %get-tuple-element.315), channel_id=1, source_target_pairs={{4,0},{8,4},{12,8},{5,1},{9,5},{13,9},{6,2},{10,6},{14,10},{7,3},{... | collective-permute-start | bytes 393224 | tf_op jit(solution)/shard_map/while/body/eval_jaxpr/ppermute | solution.py:22
  371.0 7.5 collective-permute-start
  373.0 9.3 %collective-permute-start.1 = (f32[1,64,4,128]{1,2,3,0:T(4,128)S(1)}, f32[1,64,4,128]{1,2,3,0:T(4,128)S(1)}, u32[]{:S(2)}, u32[]{:S(2)}) collective-permute-start(f32[1,64,4,128]{1,2,3,0:T(4,128)S(1)} %get-tuple-element.315), channel_id=1, source_target_pairs={{4,0},{8,4},{12,8},{5,1},{9,5},{13,9},{6,2},{10,6},{14,10},{7,3},{... | collective-permute-start | bytes 393224 | tf_op jit(solution)/shard_map/while/body/eval_jaxpr/ppermute | solution.py:22
  382.3 4.6 collective-permute-start.2
  412.8 7.5 collective-permute-start
  414.7 9.3 %collective-permute-start.1 = (f32[1,64,4,128]{1,2,3,0:T(4,128)S(1)}, f32[1,64,4,128]{1,2,3,0:T(4,128)S(1)}, u32[]{:S(2)}, u32[]{:S(2)}) collective-permute-start(f32[1,64,4,128]{1,2,3,0:T(4,128)S(1)} %get-tuple-element.315), channel_id=1, source_target_pairs={{4,0},{8,4},{12,8},{5,1},{9,5},{13,9},{6,2},{10,6},{14,10},{7,3},{... | collective-permute-start | bytes 393224 | tf_op jit(solution)/shard_map/while/body/eval_jaxpr/ppermute | solution.py:22
  454.6 7.5 collective-permute-start
  456.5 9.3 %collective-permute-start.1 = (f32[1,64,4,128]{1,2,3,0:T(4,128)S(1)}, f32[1,64,4,128]{1,2,3,0:T(4,128)S(1)}, u32[]{:S(2)}, u32[]{:S(2)}) collective-permute-start(f32[1,64,4,128]{1,2,3,0:T(4,128)S(1)} %get-tuple-element.315), channel_id=1, source_target_pairs={{4,0},{8,4},{12,8},{5,1},{9,5},{13,9},{6,2},{10,6},{14,10},{7,3},{... | collective-permute-start | bytes 393224 | tf_op jit(solution)/shard_map/while/body/eval_jaxpr/ppermute | solution.py:22
  496.4 7.5 collective-permute-start
  498.3 9.3 %collective-permute-start.1 = (f32[1,64,4,128]{1,2,3,0:T(4,128)S(1)}, f32[1,64,4,128]{1,2,3,0:T(4,128)S(1)}, u32[]{:S(2)}, u32[]{:S(2)}) collective-permute-start(f32[1,64,4,128]{1,2,3,0:T(4,128)S(1)} %get-tuple-element.315), channel_id=1, source_target_pairs={{4,0},{8,4},{12,8},{5,1},{9,5},{13,9},{6,2},{10,6},{14,10},{7,3},{... | collective-permute-start | bytes 393224 | tf_op jit(solution)/shard_map/while/body/eval_jaxpr/ppermute | solution.py:22
  507.6 4.6 collective-permute-start.2
  538.1 7.5 collective-permute-start
  540.1 9.3 %collective-permute-start.1 = (f32[1,64,4,128]{1,2,3,0:T(4,128)S(1)}, f32[1,64,4,128]{1,2,3,0:T(4,128)S(1)}, u32[]{:S(2)}, u32[]{:S(2)}) collective-permute-start(f32[1,64,4,128]{1,2,3,0:T(4,128)S(1)} %get-tuple-element.315), channel_id=1, source_target_pairs={{4,0},{8,4},{12,8},{5,1},{9,5},{13,9},{6,2},{10,6},{14,10},{7,3},{... | collective-permute-start | bytes 393224 | tf_op jit(solution)/shard_map/while/body/eval_jaxpr/ppermute | solution.py:22
  579.9 7.5 collective-permute-start
  581.8 9.3 %collective-permute-start.1 = (f32[1,64,4,128]{1,2,3,0:T(4,128)S(1)}, f32[1,64,4,128]{1,2,3,0:T(4,128)S(1)}, u32[]{:S(2)}, u32[]{:S(2)}) collective-permute-start(f32[1,64,4,128]{1,2,3,0:T(4,128)S(1)} %get-tuple-element.315), channel_id=1, source_target_pairs={{4,0},{8,4},{12,8},{5,1},{9,5},{13,9},{6,2},{10,6},{14,10},{7,3},{... | collective-permute-start | bytes 393224 | tf_op jit(solution)/shard_map/while/body/eval_jaxpr/ppermute | solution.py:22
  621.7 7.5 collective-permute-start
  623.6 9.3 %collective-permute-start.1 = (f32[1,64,4,128]{1,2,3,0:T(4,128)S(1)}, f32[1,64,4,128]{1,2,3,0:T(4,128)S(1)}, u32[]{:S(2)}, u32[]{:S(2)}) collective-permute-start(f32[1,64,4,128]{1,2,3,0:T(4,128)S(1)} %get-tuple-element.315), channel_id=1, source_target_pairs={{4,0},{8,4},{12,8},{5,1},{9,5},{13,9},{6,2},{10,6},{14,10},{7,3},{... | collective-permute-start | bytes 393224 | tf_op jit(solution)/shard_map/while/body/eval_jaxpr/ppermute | solution.py:22
  663.4 7.5 collective-permute-start
  665.4 9.3 %collective-permute-start.1 = (f32[1,64,4,128]{1,2,3,0:T(4,128)S(1)}, f32[1,64,4,128]{1,2,3,0:T(4,128)S(1)}, u32[]{:S(2)}, u32[]{:S(2)}) collective-permute-start(f32[1,64,4,128]{1,2,3,0:T(4,128)S(1)} %get-tuple-element.315), channel_id=1, source_target_pairs={{4,0},{8,4},{12,8},{5,1},{9,5},{13,9},{6,2},{10,6},{14,10},{7,3},{... | collective-permute-start | bytes 393224 | tf_op jit(solution)/shard_map/while/body/eval_jaxpr/ppermute | solution.py:22
  705.2 7.5 collective-permute-start
  707.1 9.3 %collective-permute-start.1 = (f32[1,64,4,128]{1,2,3,0:T(4,128)S(1)}, f32[1,64,4,128]{1,2,3,0:T(4,128)S(1)}, u32[]{:S(2)}, u32[]{:S(2)}) collective-permute-start(f32[1,64,4,128]{1,2,3,0:T(4,128)S(1)} %get-tuple-element.315), channel_id=1, source_target_pairs={{4,0},{8,4},{12,8},{5,1},{9,5},{13,9},{6,2},{10,6},{14,10},{7,3},{... | collective-permute-start | bytes 393224 | tf_op jit(solution)/shard_map/while/body/eval_jaxpr/ppermute | solution.py:22
  716.5 4.6 collective-permute-start.2
  747.0 7.5 collective-permute-start
  748.9 9.3 %collective-permute-start.1 = (f32[1,64,4,128]{1,2,3,0:T(4,128)S(1)}, f32[1,64,4,128]{1,2,3,0:T(4,128)S(1)}, u32[]{:S(2)}, u32[]{:S(2)}) collective-permute-start(f32[1,64,4,128]{1,2,3,0:T(4,128)S(1)} %get-tuple-element.315), channel_id=1, source_target_pairs={{4,0},{8,4},{12,8},{5,1},{9,5},{13,9},{6,2},{10,6},{14,10},{7,3},{... | collective-permute-start | bytes 393224 | tf_op jit(solution)/shard_map/while/body/eval_jaxpr/ppermute | solution.py:22
  788.8 7.5 collective-permute-start
  790.7 9.3 %collective-permute-start.1 = (f32[1,64,4,128]{1,2,3,0:T(4,128)S(1)}, f32[1,64,4,128]{1,2,3,0:T(4,128)S(1)}, u32[]{:S(2)}, u32[]{:S(2)}) collective-permute-start(f32[1,64,4,128]{1,2,3,0:T(4,128)S(1)} %get-tuple-element.315), channel_id=1, source_target_pairs={{4,0},{8,4},{12,8},{5,1},{9,5},{13,9},{6,2},{10,6},{14,10},{7,3},{... | collective-permute-start | bytes 393224 | tf_op jit(solution)/shard_map/while/body/eval_jaxpr/ppermute | solution.py:22
  830.5 7.5 collective-permute-start
  832.5 9.3 %collective-permute-start.1 = (f32[1,64,4,128]{1,2,3,0:T(4,128)S(1)}, f32[1,64,4,128]{1,2,3,0:T(4,128)S(1)}, u32[]{:S(2)}, u32[]{:S(2)}) collective-permute-start(f32[1,64,4,128]{1,2,3,0:T(4,128)S(1)} %get-tuple-element.315), channel_id=1, source_target_pairs={{4,0},{8,4},{12,8},{5,1},{9,5},{13,9},{6,2},{10,6},{14,10},{7,3},{... | collective-permute-start | bytes 393224 | tf_op jit(solution)/shard_map/while/body/eval_jaxpr/ppermute | solution.py:22
  841.8 4.6 collective-permute-start.2
  (140 other events, 462.7 us)
Sparse Core Ops, SparseCore 0:
  13.3 18.0 reduce-scatter.1
where the time goes:
time: 887 us; the launch traced here: 880 us
  local copies, waits for them, and re-layouts  413 us (47%)
  starting transfers between devices  158 us (18%)
  other arithmetic  152 us (17%)
  waiting for transfers between devices  137 us (15%)
  between operations  14.2 us (2%)
    scatter-add x20, local copies, waits for them, and re-layouts, advance(): return nxt.at[:, source_layer].add(source_now)  214 us
    add x20, other arithmetic, advance(): nxt = 2.0 * center - previous + speed[None] * laplace_inner(wide)  95.1 us
    ppermute x40, starting transfers between devices, with_halo(): lax.ppermute(lax.slice_in_dim(block, 0, width, axis=dim), axis, backward)  90.2 us
    ppermute x40, waiting for transfers between devices, with_halo(): lax.ppermute(lax.slice_in_dim(block, 0, width, axis=dim), axis, backward)  76.2 us
    while x260, local copies, waits for them, and re-layouts  72.4 us
    ppermute x40, starting transfers between devices, with_halo(): lax.ppermute(lax.slice_in_dim(block, block.shape[dim] - width, None, axis...  67.9 us
    ppermute x40, waiting for transfers between devices, with_halo(): lax.ppermute(lax.slice_in_dim(block, block.shape[dim] - width, None, axis...  46.2 us
    dynamic_update_slice x40, local copies, waits for them, and re-layouts, one_step(): record = lax.dynamic_update_index_in_dim(record, row, index, 1)  44.7 us
  transfers between devices with their start and end apart: 81, of which 60 were waited for; matrix products, arithmetic and copies ran while one was open for 9% of the time, Pallas kernels for 0%

commit v1 on v0

v1 whole, which is shorter than its diff:
```python
import functools

import jax
import jax.numpy as jnp
import ml_dtypes
from jax import lax
from jax.experimental import pallas as pl
from jax.experimental.pallas import tpu as pltpu
from jax.sharding import PartitionSpec as P

coeffs = (-205.0 / 72.0, 8.0 / 5.0, -1.0 / 5.0, 8.0 / 315.0, -1.0 / 560.0)
source_layer = 2
record_layer = 6
MESH = pl.DeviceIdType.MESH
HIGHEST = lax.Precision.HIGHEST
ROW = 8
CH = 8


def split_coeff(value):
    high = float(ml_dtypes.bfloat16(value))
    low = float(ml_dtypes.bfloat16(value - high))
    return high, low


def fill_band(ref, part):
    size = ref.shape[0]
    rows = lax.broadcasted_iota(jnp.int32, ref.shape, 0)
    cols = lax.broadcasted_iota(jnp.int32, ref.shape, 1)
    far = jnp.abs(rows - cols)
    band = jnp.zeros(ref.shape, jnp.float32)
    for j in range(1, 5):
        band = jnp.where(far == j, split_coeff(coeffs[j])[part], band)
    ref[...] = band.astype(jnp.bfloat16)


def kernel(
    n_gx,
    n_shot,
    code_ref,
    assign_ref,
    px_ref,
    py_ref,
    wav_ref,
    speed_hbm,
    press_hbm,
    prev_hbm,
    traces_hbm,
    out_hbm,
    misfit_hbm,
    field,
    speed,
    traces,
    obs,
    obs_send,
    obs_recv,
    pack,
    pack_recv,
    sources,
    record,
    record_in,
    misfit,
    band_hi,
    band_lo,
    x_send,
    x_recv,
    z_send,
    z_recv,
    load_sem,
    swap_send,
    swap_recv,
    traces_sem,
    pack_send,
    pack_rsem,
    obs_ssem,
    obs_rsem,
    rec_send,
    rec_recv,
    out_sem,
    out_send,
    out_recv,
    mis_sem,
):
    gx = lax.axis_index("gx")
    core = lax.axis_index("gy")
    shot = lax.axis_index("shot")
    depth = speed_hbm.shape[0]
    half = depth // 2
    wide = speed_hbm.shape[1]
    steps = record.shape[1]
    nsh = code_ref.shape[0]
    nchunk = half // CH
    own = pl.ds(ROW, wide)
    has_left = gx > 0
    has_right = gx < n_gx - 1
    other = 1 - core

    def shot_at(d):
        return lax.rem(shot + d, n_shot)

    def x_copy(slot, side, chunk):
        z = pl.ds(4 + CH * chunk, CH)
        if side == 0:
            src, dst, to = pl.ds(ROW, 4), pl.ds(ROW + wide, 4), gx - 1
        else:
            src, dst, to = pl.ds(ROW + wide - 4, 4), pl.ds(ROW - 4, 4), gx + 1
        return pltpu.make_async_remote_copy(
            src_ref=field.at[slot, :, z, src, :],
            dst_ref=field.at[slot, :, z, dst, :],
            send_sem=x_send.at[slot, side, chunk],
            recv_sem=x_recv.at[slot, side, chunk],
            device_id={"gx": to},
            device_id_type=MESH,
        )

    def z_copy(slot):
        src = jnp.where(core == 0, half, 4)
        dst = jnp.where(core == 0, 0, 4 + half)
        return pltpu.make_async_remote_copy(
            src_ref=field.at[slot, :, pl.ds(src, 4), own, :],
            dst_ref=field.at[slot, :, pl.ds(dst, 4), own, :],
            send_sem=z_send.at[slot],
            recv_sem=z_recv.at[slot],
            device_id={"gy": other},
            device_id_type=MESH,
        )

    def start_x(slot, chunk):
        @pl.when(has_left)
        def _():
            x_copy(slot, 0, chunk).start()

        @pl.when(has_right)
        def _():
            x_copy(slot, 1, chunk).start()

    def wait_x_recv(slot, chunk):
        @pl.when(has_right)
        def _():
            x_copy(slot, 0, chunk).wait_recv()

        @pl.when(has_left)
        def _():
            x_copy(slot, 1, chunk).wait_recv()

    def wait_x_send(slot, chunk):
        @pl.when(has_left)
        def _():
            x_copy(slot, 0, chunk).wait_send()

        @pl.when(has_right)
        def _():
            x_copy(slot, 1, chunk).wait_send()

    def place_of(which):
        if which == 0:
            return press_hbm.at[0], field.at[0, core, pl.ds(4, half), own, :]
        if which == 1:
            return speed_hbm, speed.at[core]
        return prev_hbm.at[0], field.at[1, core, pl.ds(4, half), own, :]

    def load(which):
        src, dst = place_of(which)
        return pltpu.make_async_copy(
            src.at[pl.ds(core * half, half)], dst, load_sem.at[which]
        )

    def swap(which):
        src, dst = place_of(which)
        return pltpu.make_async_remote_copy(
            src_ref=src.at[pl.ds(other * half, half)],
            dst_ref=dst,
            send_sem=swap_send.at[which],
            recv_sem=swap_recv.at[which],
            device_id={"gy": other},
            device_id_type=MESH,
        )

    def pack_copy(d):
        return pltpu.make_async_remote_copy(
            src_ref=pack,
            dst_ref=pack_recv.at[d - 1],
            send_sem=pack_send.at[d - 1],
            recv_sem=pack_rsem.at[d - 1],
            device_id={"shot": shot_at(d)},
            device_id_type=MESH,
        )

    def obs_copy(d):
        return pltpu.make_async_remote_copy(
            src_ref=obs_send.at[d - 1],
            dst_ref=obs_recv.at[d - 1],
            send_sem=obs_ssem.at[d - 1],
            recv_sem=obs_rsem.at[d - 1],
            device_id={"shot": shot_at(d)},
            device_id_type=MESH,
        )

    for which in range(3):
        load(which).start()
    traces_in = pltpu.make_async_copy(traces_hbm, traces, traces_sem)
    traces_in.start()

    for slot in range(2):
        for h in range(2):
            rows = field.shape[3]
            field[slot, h, :, 0:ROW, :] = jnp.zeros((half + 8, ROW, 128), jnp.float32)
            field[slot, h, :, ROW + wide :, :] = jnp.zeros(
                (half + 8, rows - ROW - wide, 128), jnp.float32
            )
            field[slot, h, 0:4, own, :] = jnp.zeros((4, wide, 128), jnp.float32)
            field[slot, h, 4 + half :, own, :] = jnp.zeros((4, wide, 128), jnp.float32)

    barrier = pltpu.get_barrier_semaphore()

    @pl.when(has_left)
    def _():
        pl.semaphore_signal(barrier, inc=1, device_id={"gx": gx - 1}, device_id_type=MESH)

    @pl.when(has_right)
    def _():
        pl.semaphore_signal(barrier, inc=1, device_id={"gx": gx + 1}, device_id_type=MESH)

    pl.semaphore_signal(barrier, inc=1, device_id={"gy": other}, device_id_type=MESH)
    for d in range(1, n_shot):
        pl.semaphore_signal(
            barrier, inc=1, device_id={"shot": shot_at(d)}, device_id_type=MESH
        )
    greeted = n_shot + has_left.astype(jnp.int32) + has_right.astype(jnp.int32)
    pl.semaphore_wait(barrier, greeted)

    for which in range(3):
        swap(which).start()

    lane = lax.broadcasted_iota(jnp.int32, (1, 128), 1)
    lane8 = lax.broadcasted_iota(jnp.int32, (nsh, 128), 1)
    sub8 = lax.broadcasted_iota(jnp.int32, (nsh, 128), 0)
    rows3 = [jnp.zeros((1, 128), jnp.int32) for _ in range(3)]
    signed = jnp.zeros((nsh, 128), jnp.float32)
    signs = [(2 * code_ref[s] - 1).astype(jnp.float32) for s in range(nsh)]
    for s in range(nsh):
        mine = lane == shot * nsh + s
        for r, ref in enumerate((assign_ref, px_ref, py_ref)):
            rows3[r] = jnp.where(mine, ref[s], rows3[r])
        signed = jnp.where((lane8 == shot * nsh + s) & (sub8 == s), signs[s], signed)
    pack[0:steps, :] = lax.dot_general(
        wav_ref[...], signed, (((0,), (0,)), ((), ())), precision=HIGHEST,
        preferred_element_type=jnp.float32,
    )
    for r in range(3):
        pack[steps + r : steps + r + 1, :] = rows3[r].astype(jnp.float32)
    pack[steps + 3 :, :] = jnp.zeros((pack.shape[0] - steps - 3, 128), jnp.float32)
    for d in range(1, n_shot):
        pack_copy(d).start()

    fill_band(band_hi, 0)
    fill_band(band_lo, 1)

    def chunk_of(i):
        return jnp.where(core == 0, nchunk - 1 - i, i)

    load(0).wait()
    swap(0).wait_recv()
    z_copy(0).start()
    for i in range(nchunk):
        start_x(0, chunk_of(i))

    traces_in.wait()
    for d in range(1, n_shot):
        target = shot_at(d)
        scale = [jnp.where(assign_ref[s] == target, signs[s], 0.0) for s in range(nsh)]

        def part(t, carry, scale=scale, d=d):
            total = scale[0] * traces[0, t]
            for s in range(1, nsh):
                total += scale[s] * traces[s, t]
            obs_send[d - 1, t] = total
            return carry

        lax.fori_loop(0, steps, part, 0)
        obs_copy(d).start()
    scale_own = [jnp.where(assign_ref[s] == shot, signs[s], 0.0) for s in range(nsh)]

    def part_own(t, carry):
        total = scale_own[0] * traces[0, t]
        for s in range(1, nsh):
            total += scale_own[s] * traces[s, t]
        obs[t] = total
        return carry

    lax.fori_loop(0, steps, part_own, 0)

    table = pack[...]
    for d in range(1, n_shot):
        pack_copy(d).wait_recv()
        table = table + pack_recv[d - 1]
    weight = jnp.where(
        table[steps : steps + 1] == shot.astype(jnp.float32), table[0:steps], 0.0
    )
    weight = weight * jnp.where(core == 0, 1.0, 0.0)
    local_x = table[steps + 1 : steps + 2] - (gx * wide).astype(jnp.float32)
    onex = jnp.where(
        local_x == lax.broadcasted_iota(jnp.int32, (wide, 128), 0).astype(jnp.float32), 1.0, 0.0
    )
    oney = jnp.where(
        table[steps + 2 : steps + 3]
        == lax.broadcasted_iota(jnp.int32, (256, 128), 0).astype(jnp.float32),
        1.0,
        0.0,
    )
    left = (weight[:, None, :] * onex[None]).reshape(steps * wide, 128)
    grid = lax.dot_general(
        left, oney, (((1,), (1,)), ((), ())), precision=HIGHEST,
        preferred_element_type=jnp.float32,
    )
    for h in range(2):
        sources[h] = grid[:, 128 * h : 128 * (h + 1)].reshape(steps, wide, 128)

    for which in range(1, 3):
        load(which).wait()
        swap(which).wait_recv()

    def one_chunk(n, i):
        now = lax.rem(n, 2)
        new = 1 - now
        chunk = chunk_of(i)
        z0 = 4 + CH * chunk
        zs = pl.ds(z0, CH)
        if i == 0:
            z_copy(now).wait_recv()

            @pl.when(n > 0)
            def _():
                z_copy(new).wait_send()

        wait_x_recv(now, chunk)

        @pl.when(n > 0)
        def _():
            wait_x_send(new, chunk)

        center = [field[now, h, zs, own, :] for h in range(2)]
        both = jnp.concatenate([v.reshape(CH * wide, 128) for v in center], axis=1)
        hi = both.astype(jnp.bfloat16)
        lo = (both - hi.astype(jnp.float32)).astype(jnp.bfloat16)
        dot = functools.partial(jnp.dot, preferred_element_type=jnp.float32)
        along_y = dot(hi, band_hi[...]) + dot(lo, band_hi[...]) + dot(hi, band_lo[...])
        for h in range(2):
            total = along_y[:, 128 * h : 128 * (h + 1)].reshape(CH, wide, 128)
            total = total + (3.0 * coeffs[0]) * center[h]
            for j in range(1, 5):
                ring = (
                    field[now, h, pl.ds(z0 + j, CH), own, :]
                    + field[now, h, pl.ds(z0 - j, CH), own, :]
                ) + (
                    field[now, h, zs, pl.ds(ROW + j, wide), :]
                    + field[now, h, zs, pl.ds(ROW - j, wide), :]
                )
                total = total + coeffs[j] * ring
            field[new, h, zs, own, :] = (
                2.0 * center[h] - field[new, h, zs, own, :]
                + speed[h, pl.ds(CH * chunk, CH)] * total
            )

        @pl.when((core == 0) & (chunk == 0))
        def _():
            for h in range(2):
                at = 4 + source_layer
                field[new, h, at, own, :] = field[new, h, at, own, :] + sources[h, n]
                record[h, n] = field[new, h, 4 + record_layer, own, :]

        @pl.when(n < steps - 1)
        def _():
            if i == 0:
                z_copy(new).start()
            start_x(new, chunk)

    def one_step(n, carry):
        for i in range(nchunk):
            one_chunk(n, i)
        return carry

    lax.fori_loop(0, steps, one_step, 0)

    last = steps % 2
    rest = 1 - last
    out_own = pltpu.make_async_copy(
        field.at[last, core, pl.ds(4, half), own, :],
        out_hbm.at[0, pl.ds(core * half, half)],
        out_sem,
    )
    out_own.start()
    out_away = pltpu.make_async_remote_copy(
        src_ref=field.at[last, other, pl.ds(4, half), own, :],
        dst_ref=out_hbm.at[0, pl.ds(core * half, half)],
        send_sem=out_send,
        recv_sem=out_recv,
        device_id={"gy": other},
        device_id_type=MESH,
    )
    out_away.start()
    rec_copy = pltpu.make_async_remote_copy(
        src_ref=record.at[1],
        dst_ref=record_in,
        send_sem=rec_send,
        recv_sem=rec_recv,
        device_id={"gy": other},
        device_id_type=MESH,
    )

    @pl.when(core == 0)
    def _():
        rec_copy.start()

    observed = obs[...]
    for d in range(1, n_shot):
        obs_copy(d).wait_recv()
        observed = observed + obs_recv[d - 1]

    @pl.when(core == 0)
    def _():
        misfit[...] = record[0] - observed

    @pl.when(core == 1)
    def _():
        rec_copy.wait_recv()
        misfit[...] = record_in[...] - observed

    mis = pltpu.make_async_copy(misfit, misfit_hbm.at[0], mis_sem)
    mis.start()

    z_copy(rest).wait_send()
    for i in range(nchunk):
        wait_x_send(rest, i)
    for which in range(3):
        swap(which).wait_send()
    for d in range(1, n_shot):
        pack_copy(d).wait_send()
        obs_copy(d).wait_send()

    @pl.when(core == 0)
    def _():
        rec_copy.wait_send()

    out_own.wait()
    out_away.wait()
    mis.wait()


def on_device(n_gx, n_shot, speed, pressure, previous, wavelets, traces, code, assign, px, py):
    depth, wide, wide_y = speed.shape
    nsh, steps = wavelets.shape
    half = depth // 2
    pairs = max(n_shot - 1, 1)
    f32 = jnp.float32
    smem = pl.BlockSpec(memory_space=pltpu.SMEM)
    any_ = pl.BlockSpec(memory_space=pl.ANY)
    dma = pltpu.SemaphoreType.DMA
    nchunk = half // CH
    return pl.pallas_call(
        functools.partial(kernel, n_gx, n_shot),
        out_shape=(
            jax.ShapeDtypeStruct((1, depth, wide, wide_y), f32),
            jax.ShapeDtypeStruct((1, steps, wide, wide_y), f32),
        ),
        in_specs=[smem] * 4 + [pl.BlockSpec(memory_space=pltpu.VMEM)] + [any_] * 4,
        out_specs=(any_, any_),
        scratch_shapes=[
            pltpu.VMEM((2, 2, half + 8, wide + 16, wide_y), f32),
            pltpu.VMEM((2, half, wide, wide_y), f32),
            pltpu.VMEM((nsh, steps, wide, wide_y), f32),
            pltpu.VMEM((steps, wide, wide_y), f32),
            pltpu.VMEM((pairs, steps, wide, wide_y), f32),
            pltpu.VMEM((pairs, steps, wide, wide_y), f32),
            pltpu.VMEM((-(-(steps + 3) // 8) * 8, 128), f32),
            pltpu.VMEM((pairs, -(-(steps + 3) // 8) * 8, 128), f32),
            pltpu.VMEM((2, steps, wide, wide_y), f32),
            pltpu.VMEM((2, steps, wide, wide_y), f32),
            pltpu.VMEM((steps, wide, wide_y), f32),
            pltpu.VMEM((steps, wide, wide_y), f32),
            pltpu.VMEM((2 * wide_y, 2 * wide_y), jnp.bfloat16),
            pltpu.VMEM((2 * wide_y, 2 * wide_y), jnp.bfloat16),
            dma((2, 2, nchunk)),
            dma((2, 2, nchunk)),
            dma((2,)),
            dma((2,)),
            dma((3,)),
            dma((3,)),
            dma((3,)),
            dma,
            dma((pairs,)),
            dma((pairs,)),
            dma((pairs,)),
            dma((pairs,)),
            dma,
            dma,
            dma,
            dma,
            dma,
            dma,
        ],
        compiler_params=pltpu.CompilerParams(
            collective_id=0, has_side_effects=True, vmem_limit_bytes=40 * 1024 * 1024
        ),
    )(code, assign, px, py, wavelets, speed, pressure, previous, traces)


def solution(mesh):
    return jax.shard_map(
        functools.partial(on_device, mesh.shape["gx"], mesh.shape["shot"]),
        mesh=mesh,
        in_specs=(
            P("grp", "gx", "gy"),
            P(("grp", "shot"), None, "gx", "gy"),
            P(("grp", "shot"), None, "gx", "gy"),
            P(("grp", "shot"), None),
            P(("grp", "shot"), None, "gx", "gy"),
            P(("grp", "shot")),
            P(("grp", "shot")),
            P(("grp", "shot")),
            P(("grp", "shot")),
        ),
        out_specs=(P(("grp", "shot"), None, "gx", "gy"), P(("grp", "shot"), None, "gx", "gy")),
        check_vma=False,
    )
```

time: 887 us -> 87.9 us (0.10)
  local copies, waits for them, and re-layouts: 413 us -> 9.2 us
  starting transfers between devices: 158 us -> 0 us
  other arithmetic: 152 us -> 0 us
  waiting for transfers between devices: 137 us -> 0 us
  Pallas kernels: 0 us -> 77.6 us
  between operations: 14.2 us -> 0.66 us
    scatter-add x20 -> x0, local copies, waits for them, and re-layouts: 214 us -> none  [advance(): return nxt.at[:, source_layer].add(source_now)]
    ppermute x80 -> x0, starting transfers between devices: 158 us -> none  [the longest x40 90.2 us: with_halo(): lax.ppermute(lax.slice_in_dim(block, 0, width, axis=dim), axis, backward)]
    ppermute x80 -> x0, waiting for transfers between devices: 122 us -> none  [the longest x40 76.2 us: with_halo(): lax.ppermute(lax.slice_in_dim(block, 0, width, axis=dim), axis, backward)]
    add x40 -> x0, other arithmetic: 102 us -> none  [the longest x20 95.1 us: advance(): nxt = 2.0 * center - previous + speed[None] * laplace_inner(wide)]
    pallas_call x0 -> x1, Pallas kernels: none -> 77.6 us  [on_device(): pl.pallas_call(functools.partial(kernel, n_gx, n_shot), out_shape=(jax.Sh...]
    while x263 -> x0, local copies, waits for them, and re-layouts: 76 us -> none
    dynamic_slice x60 -> x0, local copies, waits for them, and re-layouts: 71 us -> none  [the longest x40 42.6 us: one_step(): lax.dynamic_index_in_dim(observed, index, 1, keepdims=False)]
    dynamic_update_slice x40 -> x0, local copies, waits for them, and re-layouts: 44.7 us -> none  [one_step(): record = lax.dynamic_update_index_in_dim(record, row, index, 1)]
  transfers between devices with their start and end apart: 81 -> 0, of which waited for: 60 -> 0; matrix products, arithmetic and copies ran while one was open for 9% -> 0% of each run, Pallas kernels for 0% -> 0%
where the time goes in v1:
time: 87.9 us; the launch traced here: 87.5 us
  Pallas kernels  77.6 us (88%)
  local copies, waits for them, and re-layouts  9.2 us (10%)
    pallas_call x1, Pallas kernels, on_device(): pl.pallas_call(functools.partial(kernel, n_gx, n_shot), out_shape=(jax.Sh...  77.6 us
    unnamed x20, local copies, waits for them, and re-layouts  9.2 us

profile of v1, /device:TPU:1, one launch (start us, length us, event | category | flops | bytes accessed | tf_op | source)
XLA Modules:
  0.0 87.5 jit_solution(13295667209346045422)
XLA Ops:
  0.6 0.0 copy-start
  0.6 1.3 %copy-done = f32[8,20,16,128]{3,2,1,0:T(8,128)S(1)} copy-done((f32[8,20,16,128]{3,2,1,0:T(8,128)S(1)}, f32[8,20,16,128]{3,2,1,0:T(8,128)}, u32[]{:S(2)}) %copy-start) | copy-done | bytes 1310744
  2.0 0.0 copy-start.1
  2.0 1.0 %copy-done.1 = f32[64,16,128]{2,1,0:T(8,128)S(1)} copy-done((f32[64,16,128]{2,1,0:T(8,128)S(1)}, f32[64,16,128]{2,1,0:T(8,128)}, u32[]{:S(2)}) %copy-start.1) | copy-done | bytes 524312
  3.0 0.0 copy-start.2
  3.0 1.0 %copy-done.2 = f32[1,64,16,128]{3,2,1,0:T(8,128)S(1)} copy-done((f32[1,64,16,128]{3,2,1,0:T(8,128)S(1)}, f32[1,64,16,128]{3,2,1,0:T(8,128)}, u32[]{:S(2)}) %copy-start.2) | copy-done | bytes 524312
  4.0 0.0 copy-start.3
  4.0 1.0 %copy-done.3 = f32[1,64,16,128]{3,2,1,0:T(8,128)S(1)} copy-done((f32[1,64,16,128]{3,2,1,0:T(8,128)S(1)}, f32[1,64,16,128]{3,2,1,0:T(8,128)}, u32[]{:S(2)}) %copy-start.3) | copy-done | bytes 524312
  5.1 0.0 copy-start.4
  5.1 0.7 copy-done.4
  5.8 0.0 copy-start.5
  5.8 0.7 copy-done.5
  6.4 0.0 copy-start.6
  6.4 0.7 copy-done.6
  7.1 0.0 copy-start.7
  7.1 0.7 copy-done.7
  7.7 0.0 copy-start.8
  7.7 0.7 copy-done.8
  8.4 77.6 %shard_map.104 = (f32[1,64,16,128]{3,2,1,0:T(8,128)S(1)}, f32[1,20,16,128]{3,2,1,0:T(8,128)S(1)}) custom-call(s32[8]{0:T(128)S(1)} %copy-done.5, s32[8]{0:T(128)S(1)} %copy-done.6, s32[8]{0:T(128)S(1)} %copy-done.7, s32[8]{0:T(128)S(1)} %copy-done.8, f32[8,20]{1,0:T(8,128)S(1)} %copy-done.4, f32[64,16,128]{2,1,0:T(8,128)S(1)} %copy-done.1, ...), custom_call_target="tpu_custom_call" | custom-call | tf_op jit(solution)/shard_map/pallas_call | solution.py:460
  86.0 0.8 copy.13
  86.8 0.7 copy.14
Async XLA Ops:
  0.6 1.3 %copy-start = (f32[8,20,16,128]{3,2,1,0:T(8,128)S(1)}, f32[8,20,16,128]{3,2,1,0:T(8,128)}, u32[]{:S(2)}) copy-start(f32[8,20,16,128]{3,2,1,0:T(8,128)} %traces_hbm.1) | copy-start | bytes 3932164
  2.0 1.0 %copy-start.1 = (f32[64,16,128]{2,1,0:T(8,128)S(1)}, f32[64,16,128]{2,1,0:T(8,128)}, u32[]{:S(2)}) copy-start(f32[64,16,128]{2,1,0:T(8,128)} %speed_hbm.1) | copy-start | bytes 1572868
  3.0 1.0 %copy-start.2 = (f32[1,64,16,128]{3,2,1,0:T(8,128)S(1)}, f32[1,64,16,128]{3,2,1,0:T(8,128)}, u32[]{:S(2)}) copy-start(f32[1,64,16,128]{3,2,1,0:T(8,128)} %press_hbm.1) | copy-start | bytes 1572868
  4.0 1.0 %copy-start.3 = (f32[1,64,16,128]{3,2,1,0:T(8,128)S(1)}, f32[1,64,16,128]{3,2,1,0:T(8,128)}, u32[]{:S(2)}) copy-start(f32[1,64,16,128]{3,2,1,0:T(8,128)} %prev_hbm.1) | copy-start | bytes 1572868
  5.1 0.7 copy-start.4
  5.8 0.7 copy-start.5
  6.4 0.7 copy-start.6
  7.1 0.7 copy-start.7
  7.7 0.7 copy-start.8

commit v2 on v1

--- a/solution.py
+++ b/solution.py
@@ -14,7 +14,7 @@
 MESH = pl.DeviceIdType.MESH
 HIGHEST = lax.Precision.HIGHEST
 ROW = 8
-CH = 8
+CH = 4
 
 
 def split_coeff(value):
@@ -37,17 +37,22 @@
 def kernel(
     n_gx,
     n_shot,
-    code_ref,
-    assign_ref,
-    px_ref,
-    py_ref,
-    wav_ref,
+    code_hbm,
+    assign_hbm,
+    px_hbm,
+    py_hbm,
+    wav_hbm,
     speed_hbm,
     press_hbm,
     prev_hbm,
     traces_hbm,
     out_hbm,
     misfit_hbm,
+    code_ref,
+    assign_ref,
+    px_ref,
+    py_ref,
+    wav_ref,
     field,
     speed,
     traces,
@@ -70,6 +75,8 @@
     swap_send,
     swap_recv,
     traces_sem,
+    small_sem,
+    init_send,
     pack_send,
     pack_rsem,
     obs_ssem,
@@ -89,6 +96,8 @@
     wide = speed_hbm.shape[1]
     steps = record.shape[1]
     nsh = code_ref.shape[0]
+    last = steps % 2
+    rest = 1 - last
     nchunk = half // CH
     own = pl.ds(ROW, wide)
     has_left = gx > 0
@@ -152,26 +161,81 @@
         def _():
             x_copy(slot, 1, chunk).wait_send()
 
-    def place_of(which):
+    def place_of(which, to):
         if which == 0:
-            return press_hbm.at[0], field.at[0, core, pl.ds(4, half), own, :]
+            src = press_hbm.at[0, pl.ds(to * (half - 4), half + 4)]
+            return src, field.at[0, core, pl.ds(4 * (1 - to), half + 4), own, :]
         if which == 1:
-            return speed_hbm, speed.at[core]
-        return prev_hbm.at[0], field.at[1, core, pl.ds(4, half), own, :]
+            return speed_hbm.at[pl.ds(to * half, half)], speed.at[core]
+        src = prev_hbm.at[0, pl.ds(to * half, half)]
+        return src, field.at[1, core, pl.ds(4, half), own, :]
 
     def load(which):
-        src, dst = place_of(which)
-        return pltpu.make_async_copy(
-            src.at[pl.ds(core * half, half)], dst, load_sem.at[which]
-        )
+        src, dst = place_of(which, core)
+        return pltpu.make_async_copy(src, dst, load_sem.at[which])
 
     def swap(which):
-        src, dst = place_of(which)
-        return pltpu.make_async_remote_copy(
-            src_ref=src.at[pl.ds(other * half, half)],
+        src, dst = place_of(which, other)
+        return pltpu.make_async_remote_copy(
+            src_ref=src,
             dst_ref=dst,
             send_sem=swap_send.at[which],
             recv_sem=swap_recv.at[which],
+            device_id={"gy": other},
+            device_id_type=MESH,
+        )
+
+    def init_copy(side, to, chunk):
+        if side == 0:
+            src, dst, nb = pl.ds(0, 4), pl.ds(ROW + wide, 4), gx - 1
+        else:
+            src, dst, nb = pl.ds(wide - 4, 4), pl.ds(ROW - 4, 4), gx + 1
+        index = jnp.where(to == 0, nchunk - 1 - chunk, chunk)
+        return pltpu.make_async_remote_copy(
+            src_ref=press_hbm.at[0, pl.ds(to * half + CH * index, CH), src, :],
+            dst_ref=field.at[0, core, pl.ds(4 + CH * index, CH), dst, :],
+            send_sem=init_send.at[side, jnp.where(to == core, 0, 1), chunk],
+            recv_sem=x_recv.at[0, side, index],
+            device_id={"gx": nb, "gy": to},
+            device_id_type=MESH,
+        )
+
+    def each_init(act):
+        for chunk in range(nchunk):
+            for to in (core, other):
+
+                @pl.when(has_left)
+                def _(chunk=chunk, to=to):
+                    act(init_copy(0, to, chunk))
+
+                @pl.when(has_right)
+                def _(chunk=chunk, to=to):
+                    act(init_copy(1, to, chunk))
+
+    def out_copy(chunk):
+        return pltpu.make_async_copy(
+            field.at[last, core, pl.ds(4 + CH * chunk, CH), own, :],
+            out_hbm.at[0, pl.ds(core * half + CH * chunk, CH)],
+            out_sem.at[chunk],
+        )
+
+    def out_away(chunk):
+        return pltpu.make_async_remote_copy(
+            src_ref=field.at[last, other, pl.ds(4 + CH * chunk, CH), own, :],
+            dst_ref=out_hbm.at[0, pl.ds(core * half + CH * chunk, CH)],
+            send_sem=out_send.at[chunk],
+            recv_sem=out_recv.at[chunk],
+            device_id={"gy": other},
+            device_id_type=MESH,
+        )
+
+    def rec_copy(which):
+        rows = pl.ds(0, steps - 1) if which == 0 else pl.ds(steps - 1, 1)
+        return pltpu.make_async_remote_copy(
+            src_ref=record.at[1, rows],
+            dst_ref=record_in.at[rows],
+            send_sem=rec_send.at[which],
+            recv_sem=rec_recv.at[which],
             device_id={"gy": other},
             device_id_type=MESH,
         )
@@ -196,41 +260,68 @@
             device_id_type=MESH,
         )
 
+    barrier = pltpu.get_barrier_semaphore()
+
+    def greet(device):
+        pl.semaphore_signal(barrier, inc=1, device_id=device, device_id_type=MESH)
+
+    @pl.when(has_left)
+    def _():
+        for to in (core, other):
+            greet({"gx": gx - 1, "gy": to})
+
+    @pl.when(has_right)
+    def _():
+        for to in (core, other):
+            greet({"gx": gx + 1, "gy": to})
+
+    greet({"gy": other})
+    for d in range(1, n_shot):
+        greet({"shot": shot_at(d)})
+
+    small = [
+        pltpu.make_async_copy(src, dst, small_sem.at[i])
+        for i, (src, dst) in enumerate(
+            (
+                (code_hbm, code_ref),
+                (assign_hbm, assign_ref),
+                (px_hbm, px_ref),
+                (py_hbm, py_ref),
+                (wav_hbm, wav_ref),
+            )
+        )
+    ]
+    for copy in small:
+        copy.start()
     for which in range(3):
         load(which).start()
     traces_in = pltpu.make_async_copy(traces_hbm, traces, traces_sem)
     traces_in.start()
 
+    greeted = n_shot + 2 * (has_left.astype(jnp.int32) + has_right.astype(jnp.int32))
+    pl.semaphore_wait(barrier, greeted)
+    swap(0).start()
+    each_init(lambda copy: copy.start())
+    for which in (1, 2):
+        swap(which).start()
+
     for slot in range(2):
         for h in range(2):
-            rows = field.shape[3]
-            field[slot, h, :, 0:ROW, :] = jnp.zeros((half + 8, ROW, 128), jnp.float32)
-            field[slot, h, :, ROW + wide :, :] = jnp.zeros(
-                (half + 8, rows - ROW - wide, 128), jnp.float32
+
+            @pl.when(jnp.logical_not(has_left))
+            def _(slot=slot, h=h):
+                field[slot, h, :, 0:ROW, :] = jnp.zeros((half + 8, ROW, 128), jnp.float32)
+
+            @pl.when(jnp.logical_not(has_right))
+            def _(slot=slot, h=h):
+                field[slot, h, :, ROW + wide :, :] = jnp.zeros((half + 8, 8, 128), jnp.float32)
+
+            field[slot, h, pl.ds(core * (half + 4), 4), own, :] = jnp.zeros(
+                (4, wide, 128), jnp.float32
             )
-            field[slot, h, 0:4, own, :] = jnp.zeros((4, wide, 128), jnp.float32)
-            field[slot, h, 4 + half :, own, :] = jnp.zeros((4, wide, 128), jnp.float32)
-
-    barrier = pltpu.get_barrier_semaphore()
-
-    @pl.when(has_left)
-    def _():
-        pl.semaphore_signal(barrier, inc=1, device_id={"gx": gx - 1}, device_id_type=MESH)
-
-    @pl.when(has_right)
-    def _():
-        pl.semaphore_signal(barrier, inc=1, device_id={"gx": gx + 1}, device_id_type=MESH)
-
-    pl.semaphore_signal(barrier, inc=1, device_id={"gy": other}, device_id_type=MESH)
-    for d in range(1, n_shot):
-        pl.semaphore_signal(
-            barrier, inc=1, device_id={"shot": shot_at(d)}, device_id_type=MESH
-        )
-    greeted = n_shot + has_left.astype(jnp.int32) + has_right.astype(jnp.int32)
-    pl.semaphore_wait(barrier, greeted)
-
-    for which in range(3):
-        swap(which).start()
+
+    for copy in small:
+        copy.wait()
 
     lane = lax.broadcasted_iota(jnp.int32, (1, 128), 1)
     lane8 = lax.broadcasted_iota(jnp.int32, (nsh, 128), 1)
@@ -259,36 +350,24 @@
     def chunk_of(i):
         return jnp.where(core == 0, nchunk - 1 - i, i)
 
-    load(0).wait()
-    swap(0).wait_recv()
-    z_copy(0).start()
-    for i in range(nchunk):
-        start_x(0, chunk_of(i))
-
-    traces_in.wait()
-    for d in range(1, n_shot):
-        target = shot_at(d)
-        scale = [jnp.where(assign_ref[s] == target, signs[s], 0.0) for s in range(nsh)]
-
-        def part(t, carry, scale=scale, d=d):
-            total = scale[0] * traces[0, t]
-            for s in range(1, nsh):
-                total += scale[s] * traces[s, t]
-            obs_send[d - 1, t] = total
-            return carry
-
-        lax.fori_loop(0, steps, part, 0)
-        obs_copy(d).start()
-    scale_own = [jnp.where(assign_ref[s] == shot, signs[s], 0.0) for s in range(nsh)]
-
-    def part_own(t, carry):
-        total = scale_own[0] * traces[0, t]
-        for s in range(1, nsh):
-            total += scale_own[s] * traces[s, t]
-        obs[t] = total
-        return carry
-
-    lax.fori_loop(0, steps, part_own, 0)
+    owners = [shot_at(d) for d in range(n_shot)]
+    scales = [
+        [jnp.where(assign_ref[k] == owner, signs[k], 0.0) for k in range(nsh)]
+        for owner in owners
+    ]
+
+    def encode_rows(first, count):
+        for r in range(count):
+            t = first + r
+            rows = [traces[k, t] for k in range(nsh)]
+            for d in range(n_shot):
+                total = scales[d][0] * rows[0]
+                for k in range(1, nsh):
+                    total += scales[d][k] * rows[k]
+                if d == 0:
+                    obs[t] = total
+                else:
+                    obs_send[d - 1, t] = total
 
     table = pack[...]
     for d in range(1, n_shot):
@@ -316,9 +395,10 @@
     for h in range(2):
         sources[h] = grid[:, 128 * h : 128 * (h + 1)].reshape(steps, wide, 128)
 
-    for which in range(1, 3):
+    for which in range(3):
         load(which).wait()
         swap(which).wait_recv()
+    traces_in.wait()
 
     def one_chunk(n, i):
         now = lax.rem(n, 2)
@@ -327,15 +407,18 @@
         z0 = 4 + CH * chunk
         zs = pl.ds(z0, CH)
         if i == 0:
-            z_copy(now).wait_recv()
 
             @pl.when(n > 0)
             def _():
+                z_copy(now).wait_recv()
+
+            @pl.when(n > 1)
+            def _():
                 z_copy(new).wait_send()
 
         wait_x_recv(now, chunk)
 
-        @pl.when(n > 0)
+        @pl.when(n > 1)
         def _():
             wait_x_send(new, chunk)
 
@@ -375,42 +458,38 @@
                 z_copy(new).start()
             start_x(new, chunk)
 
+        @pl.when(n == steps - 1)
+        def _():
+            out_away(chunk).start()
+            out_copy(chunk).start()
+
+    batch = 2
+    encoding = -(-steps // batch)
+
     def one_step(n, carry):
         for i in range(nchunk):
             one_chunk(n, i)
+
+        @pl.when(n < encoding)
+        def _():
+            encode_rows(n * batch, batch)
+
+        @pl.when(n == encoding)
+        def _():
+            for d in range(1, n_shot):
+                obs_copy(d).start()
+
+        @pl.when((n == steps - 2) & (core == 0))
+        def _():
+            rec_copy(0).start()
+
         return carry
 
     lax.fori_loop(0, steps, one_step, 0)
-
-    last = steps % 2
-    rest = 1 - last
-    out_own = pltpu.make_async_copy(
-        field.at[last, core, pl.ds(4, half), own, :],
-        out_hbm.at[0, pl.ds(core * half, half)],
-        out_sem,
-    )
-    out_own.start()
-    out_away = pltpu.make_async_remote_copy(
-        src_ref=field.at[last, other, pl.ds(4, half), own, :],
-        dst_ref=out_hbm.at[0, pl.ds(core * half, half)],
-        send_sem=out_send,
-        recv_sem=out_recv,
-        device_id={"gy": other},
-        device_id_type=MESH,
-    )
-    out_away.start()
-    rec_copy = pltpu.make_async_remote_copy(
-        src_ref=record.at[1],
-        dst_ref=record_in,
-        send_sem=rec_send,
-        recv_sem=rec_recv,
-        device_id={"gy": other},
-        device_id_type=MESH,
-    )
 
     @pl.when(core == 0)
     def _():
-        rec_copy.start()
+        rec_copy(1).start()
 
     observed = obs[...]
     for d in range(1, n_shot):
@@ -423,7 +502,8 @@
 
     @pl.when(core == 1)
     def _():
-        rec_copy.wait_recv()
+        rec_copy(0).wait_recv()
+        rec_copy(1).wait_recv()
         misfit[...] = record_in[...] - observed
 
     mis = pltpu.make_async_copy(misfit, misfit_hbm.at[0], mis_sem)
@@ -440,10 +520,13 @@
 
     @pl.when(core == 0)
     def _():
-        rec_copy.wait_send()
-
-    out_own.wait()
-    out_away.wait()
+        rec_copy(0).wait_send()
+        rec_copy(1).wait_send()
+
+    each_init(lambda copy: copy.wait_send())
+    for chunk in range(nchunk):
+        out_copy(chunk).wait()
+        out_away(chunk).wait()
     mis.wait()
 
 
@@ -453,8 +536,7 @@
     half = depth // 2
     pairs = max(n_shot - 1, 1)
     f32 = jnp.float32
-    smem = pl.BlockSpec(memory_space=pltpu.SMEM)
-    any_ = pl.BlockSpec(memory_space=pl.ANY)
+    hbm = pl.BlockSpec(memory_space=pltpu.HBM)
     dma = pltpu.SemaphoreType.DMA
     nchunk = half // CH
     return pl.pallas_call(
@@ -463,9 +545,14 @@
             jax.ShapeDtypeStruct((1, depth, wide, wide_y), f32),
             jax.ShapeDtypeStruct((1, steps, wide, wide_y), f32),
         ),
-        in_specs=[smem] * 4 + [pl.BlockSpec(memory_space=pltpu.VMEM)] + [any_] * 4,
-        out_specs=(any_, any_),
+        in_specs=[hbm] * 9,
+        out_specs=(hbm, hbm),
         scratch_shapes=[
+            pltpu.SMEM((nsh,), jnp.int32),
+            pltpu.SMEM((nsh,), jnp.int32),
+            pltpu.SMEM((nsh,), jnp.int32),
+            pltpu.SMEM((nsh,), jnp.int32),
+            pltpu.VMEM((nsh, steps), f32),
             pltpu.VMEM((2, 2, half + 8, wide + 16, wide_y), f32),
             pltpu.VMEM((2, half, wide, wide_y), f32),
             pltpu.VMEM((nsh, steps, wide, wide_y), f32),
@@ -488,19 +575,21 @@
             dma((3,)),
             dma((3,)),
             dma,
+            dma((5,)),
+            dma((2, 2, nchunk)),
             dma((pairs,)),
             dma((pairs,)),
             dma((pairs,)),
             dma((pairs,)),
-            dma,
-            dma,
-            dma,
-            dma,
-            dma,
+            dma((2,)),
+            dma((2,)),
+            dma((nchunk,)),
+            dma((nchunk,)),
+            dma((nchunk,)),
             dma,
         ],
         compiler_params=pltpu.CompilerParams(
-            collective_id=0, has_side_effects=True, vmem_limit_bytes=40 * 1024 * 1024
+            collective_id=0, has_side_effects=True, vmem_limit_bytes=62 * 1024 * 1024
         ),
     )(code, assign, px, py, wavelets, speed, pressure, previous, traces)
 

time: 87.9 us -> 78 us (0.89)
  local copies, waits for them, and re-layouts: 9.2 us -> 3.46 us
  Pallas kernels: 77.6 us -> 73.7 us
    unnamed x20 -> x2, local copies, waits for them, and re-layouts: 9.2 us -> 3.46 us
    pallas_call x1, Pallas kernels: 77.6 us -> 73.7 us  [on_device(): pl.pallas_call(functools.partial(kernel, n_gx, n_shot), out_shape=(jax.Sh...]
where the time goes in v2:
time: 78 us; the launch traced here: 77.8 us
  Pallas kernels  73.7 us (94%)
  local copies, waits for them, and re-layouts  3.46 us (4%)
    pallas_call x1, Pallas kernels, on_device(): pl.pallas_call(functools.partial(kernel, n_gx, n_shot), out_shape=(jax.Sh...  73.7 us
    unnamed x2, local copies, waits for them, and re-layouts  3.46 us

profile of v2, /device:TPU:1, one launch (start us, length us, event | category | flops | bytes accessed | tf_op | source)
XLA Modules:
  0.0 77.8 jit_solution(13327010258406825150)
XLA Ops:
  0.6 73.7 %shard_map.104 = (f32[1,64,16,128]{3,2,1,0:T(8,128)}, f32[1,20,16,128]{3,2,1,0:T(8,128)}) custom-call(s32[8]{0:T(128)} %code_hbm.1, s32[8]{0:T(128)} %assign_hbm.1, s32[8]{0:T(128)} %px_hbm.1, s32[8]{0:T(128)} %py_hbm.1, f32[8,20]{1,0:T(8,128)} %wav_hbm.1, f32[64,16,128]{2,1,0:T(8,128)} %speed_hbm.1, f32[1,64,16,128]{3,2,1,0:T(8,128)} %press_hbm.1, ...), custom_call_target="tpu_custom_call" | custom-call | tf_op jit(solution)/shard_map/pallas_call | solution.py:542
  74.4 1.9 %copy.13 = f32[1,64,16,128]{3,2,1,0:T(8,128)} copy(f32[1,64,16,128]{3,2,1,0:T(8,128)} %get-tuple-element.4) | data formatting | bytes 1048576
  76.2 1.6 %copy.14 = f32[1,20,16,128]{3,2,1,0:T(8,128)} copy(f32[1,20,16,128]{3,2,1,0:T(8,128)} %get-tuple-element.5) | data formatting | bytes 327680

commit v3 on v2

--- a/solution.py
+++ b/solution.py
@@ -369,36 +369,35 @@
                 else:
                     obs_send[d - 1, t] = total
 
-    table = pack[...]
-    for d in range(1, n_shot):
-        pack_copy(d).wait_recv()
-        table = table + pack_recv[d - 1]
-    weight = jnp.where(
-        table[steps : steps + 1] == shot.astype(jnp.float32), table[0:steps], 0.0
-    )
-    weight = weight * jnp.where(core == 0, 1.0, 0.0)
-    local_x = table[steps + 1 : steps + 2] - (gx * wide).astype(jnp.float32)
-    onex = jnp.where(
-        local_x == lax.broadcasted_iota(jnp.int32, (wide, 128), 0).astype(jnp.float32), 1.0, 0.0
-    )
-    oney = jnp.where(
-        table[steps + 2 : steps + 3]
-        == lax.broadcasted_iota(jnp.int32, (256, 128), 0).astype(jnp.float32),
-        1.0,
-        0.0,
-    )
-    left = (weight[:, None, :] * onex[None]).reshape(steps * wide, 128)
-    grid = lax.dot_general(
-        left, oney, (((1,), (1,)), ((), ())), precision=HIGHEST,
-        preferred_element_type=jnp.float32,
-    )
-    for h in range(2):
-        sources[h] = grid[:, 128 * h : 128 * (h + 1)].reshape(steps, wide, 128)
-
     for which in range(3):
         load(which).wait()
         swap(which).wait_recv()
     traces_in.wait()
+
+    def make_sources():
+        table = pack[...]
+        for d in range(1, n_shot):
+            table = table + pack_recv[d - 1]
+        weight = jnp.where(
+            table[steps : steps + 1] == shot.astype(jnp.float32), table[0:steps], 0.0
+        )
+        local_x = table[steps + 1 : steps + 2] - (gx * wide).astype(jnp.float32)
+        onex = jnp.where(
+            local_x == lax.broadcasted_iota(jnp.int32, (wide, 128), 0).astype(jnp.float32), 1.0, 0.0
+        )
+        oney = jnp.where(
+            table[steps + 2 : steps + 3]
+            == lax.broadcasted_iota(jnp.int32, (256, 128), 0).astype(jnp.float32),
+            1.0,
+            0.0,
+        )
+        left = (weight[:, None, :] * onex[None]).reshape(steps * wide, 128)
+        grid = lax.dot_general(
+            left, oney, (((1,), (1,)), ((), ())), precision=HIGHEST,
+            preferred_element_type=jnp.float32,
+        )
+        for h in range(2):
+            sources[h] = grid[:, 128 * h : 128 * (h + 1)].reshape(steps, wide, 128)
 
     def one_chunk(n, i):
         now = lax.rem(n, 2)
@@ -416,32 +415,49 @@
             def _():
                 z_copy(new).wait_send()
 
-        wait_x_recv(now, chunk)
-
-        @pl.when(n > 1)
-        def _():
-            wait_x_send(new, chunk)
-
         center = [field[now, h, zs, own, :] for h in range(2)]
         both = jnp.concatenate([v.reshape(CH * wide, 128) for v in center], axis=1)
         hi = both.astype(jnp.bfloat16)
         lo = (both - hi.astype(jnp.float32)).astype(jnp.bfloat16)
         dot = functools.partial(jnp.dot, preferred_element_type=jnp.float32)
         along_y = dot(hi, band_hi[...]) + dot(lo, band_hi[...]) + dot(hi, band_lo[...])
+        totals = []
         for h in range(2):
             total = along_y[:, 128 * h : 128 * (h + 1)].reshape(CH, wide, 128)
             total = total + (3.0 * coeffs[0]) * center[h]
             for j in range(1, 5):
-                ring = (
+                total = total + coeffs[j] * (
                     field[now, h, pl.ds(z0 + j, CH), own, :]
                     + field[now, h, pl.ds(z0 - j, CH), own, :]
-                ) + (
+                )
+            totals.append(total)
+
+        if i == nchunk - 1:
+
+            @pl.when(n == 0)
+            def _():
+                for d in range(1, n_shot):
+                    pack_copy(d).wait_recv()
+
+                @pl.when(core == 0)
+                def _():
+                    make_sources()
+
+        @pl.when(n > 1)
+        def _():
+            wait_x_send(new, chunk)
+
+        wait_x_recv(now, chunk)
+
+        for h in range(2):
+            total = totals[h]
+            for j in range(1, 5):
+                total = total + coeffs[j] * (
                     field[now, h, zs, pl.ds(ROW + j, wide), :]
                     + field[now, h, zs, pl.ds(ROW - j, wide), :]
                 )
-                total = total + coeffs[j] * ring
             field[new, h, zs, own, :] = (
-                2.0 * center[h] - field[new, h, zs, own, :]
+                2.0 * field[now, h, zs, own, :] - field[new, h, zs, own, :]
                 + speed[h, pl.ds(CH * chunk, CH)] * total
             )
 
@@ -491,23 +507,30 @@
     def _():
         rec_copy(1).start()
 
-    observed = obs[...]
+    def mis_copy(which):
+        rows = pl.ds(0, steps - 1) if which == 0 else pl.ds(steps - 1, 1)
+        return pltpu.make_async_copy(
+            misfit.at[rows], misfit_hbm.at[0, rows], mis_sem.at[which]
+        )
+
     for d in range(1, n_shot):
         obs_copy(d).wait_recv()
-        observed = observed + obs_recv[d - 1]
-
-    @pl.when(core == 0)
-    def _():
-        misfit[...] = record[0] - observed
-
-    @pl.when(core == 1)
-    def _():
-        rec_copy(0).wait_recv()
-        rec_copy(1).wait_recv()
-        misfit[...] = record_in[...] - observed
-
-    mis = pltpu.make_async_copy(misfit, misfit_hbm.at[0], mis_sem)
-    mis.start()
+    for which in range(2):
+        rows = pl.ds(0, steps - 1) if which == 0 else pl.ds(steps - 1, 1)
+        observed = obs[rows]
+        for d in range(1, n_shot):
+            observed = observed + obs_recv[d - 1, rows]
+
+        @pl.when(core == 0)
+        def _(rows=rows, observed=observed):
+            misfit[rows] = record[0, rows] - observed
+
+        @pl.when(core == 1)
+        def _(which=which, rows=rows, observed=observed):
+            rec_copy(which).wait_recv()
+            misfit[rows] = record_in[rows] - observed
+
+        mis_copy(which).start()
 
     z_copy(rest).wait_send()
     for i in range(nchunk):
@@ -527,7 +550,8 @@
     for chunk in range(nchunk):
         out_copy(chunk).wait()
         out_away(chunk).wait()
-    mis.wait()
+    for which in range(2):
+        mis_copy(which).wait()
 
 
 def on_device(n_gx, n_shot, speed, pressure, previous, wavelets, traces, code, assign, px, py):
@@ -586,7 +610,7 @@
             dma((nchunk,)),
             dma((nchunk,)),
             dma((nchunk,)),
-            dma,
+            dma((2,)),
         ],
         compiler_params=pltpu.CompilerParams(
             collective_id=0, has_side_effects=True, vmem_limit_bytes=62 * 1024 * 1024

time: 78 us -> 75.7 us (0.971)
  Pallas kernels: 73.7 us -> 71.4 us
    pallas_call x1, Pallas kernels: 73.7 us -> 71.4 us  [on_device(): pl.pallas_call(functools.partial(kernel, n_gx, n_shot), out_shape=(jax.Sh...]
where the time goes in v3:
time: 75.7 us; the launch traced here: 75.5 us
  Pallas kernels  71.4 us (94%)
  local copies, waits for them, and re-layouts  3.46 us (5%)
    pallas_call x1, Pallas kernels, on_device(): pl.pallas_call(functools.partial(kernel, n_gx, n_shot), out_shape=(jax.Sh...  71.4 us
    unnamed x2, local copies, waits for them, and re-layouts  3.46 us

profile of v3, /device:TPU:1, one launch (start us, length us, event | category | flops | bytes accessed | tf_op | source)
XLA Modules:
  0.0 75.5 jit_solution(15305530384806784991)
XLA Ops:
  0.6 71.4 %shard_map.104 = (f32[1,64,16,128]{3,2,1,0:T(8,128)}, f32[1,20,16,128]{3,2,1,0:T(8,128)}) custom-call(s32[8]{0:T(128)} %code_hbm.1, s32[8]{0:T(128)} %assign_hbm.1, s32[8]{0:T(128)} %px_hbm.1, s32[8]{0:T(128)} %py_hbm.1, f32[8,20]{1,0:T(8,128)} %wav_hbm.1, f32[64,16,128]{2,1,0:T(8,128)} %speed_hbm.1, f32[1,64,16,128]{3,2,1,0:T(8,128)} %press_hbm.1, ...), custom_call_target="tpu_custom_call" | custom-call | tf_op jit(solution)/shard_map/pallas_call | solution.py:566
  72.1 1.9 %copy.13 = f32[1,64,16,128]{3,2,1,0:T(8,128)} copy(f32[1,64,16,128]{3,2,1,0:T(8,128)} %get-tuple-element.4) | data formatting | bytes 1048576
  73.9 1.6 %copy.14 = f32[1,20,16,128]{3,2,1,0:T(8,128)} copy(f32[1,20,16,128]{3,2,1,0:T(8,128)} %get-tuple-element.5) | data formatting | bytes 327680

commit v4 on v3

--- a/solution.py
+++ b/solution.py
@@ -298,6 +298,24 @@
     traces_in = pltpu.make_async_copy(traces_hbm, traces, traces_sem)
     traces_in.start()
 
+    for slot in range(2):
+        for h in range(2):
+
+            @pl.when(jnp.logical_not(has_left))
+            def _(slot=slot, h=h):
+                field[slot, h, :, 0:ROW, :] = jnp.zeros((half + 8, ROW, 128), jnp.float32)
+
+            @pl.when(jnp.logical_not(has_right))
+            def _(slot=slot, h=h):
+                field[slot, h, :, ROW + wide :, :] = jnp.zeros((half + 8, 8, 128), jnp.float32)
+
+            field[slot, h, pl.ds(core * (half + 4), 4), own, :] = jnp.zeros(
+                (4, wide, 128), jnp.float32
+            )
+
+    fill_band(band_hi, 0)
+    fill_band(band_lo, 1)
+
     greeted = n_shot + 2 * (has_left.astype(jnp.int32) + has_right.astype(jnp.int32))
     pl.semaphore_wait(barrier, greeted)
     swap(0).start()
@@ -305,58 +323,43 @@
     for which in (1, 2):
         swap(which).start()
 
-    for slot in range(2):
-        for h in range(2):
-
-            @pl.when(jnp.logical_not(has_left))
-            def _(slot=slot, h=h):
-                field[slot, h, :, 0:ROW, :] = jnp.zeros((half + 8, ROW, 128), jnp.float32)
-
-            @pl.when(jnp.logical_not(has_right))
-            def _(slot=slot, h=h):
-                field[slot, h, :, ROW + wide :, :] = jnp.zeros((half + 8, 8, 128), jnp.float32)
-
-            field[slot, h, pl.ds(core * (half + 4), 4), own, :] = jnp.zeros(
-                (4, wide, 128), jnp.float32
-            )
-
-    for copy in small:
-        copy.wait()
-
-    lane = lax.broadcasted_iota(jnp.int32, (1, 128), 1)
-    lane8 = lax.broadcasted_iota(jnp.int32, (nsh, 128), 1)
-    sub8 = lax.broadcasted_iota(jnp.int32, (nsh, 128), 0)
-    rows3 = [jnp.zeros((1, 128), jnp.int32) for _ in range(3)]
-    signed = jnp.zeros((nsh, 128), jnp.float32)
-    signs = [(2 * code_ref[s] - 1).astype(jnp.float32) for s in range(nsh)]
-    for s in range(nsh):
-        mine = lane == shot * nsh + s
-        for r, ref in enumerate((assign_ref, px_ref, py_ref)):
-            rows3[r] = jnp.where(mine, ref[s], rows3[r])
-        signed = jnp.where((lane8 == shot * nsh + s) & (sub8 == s), signs[s], signed)
-    pack[0:steps, :] = lax.dot_general(
-        wav_ref[...], signed, (((0,), (0,)), ((), ())), precision=HIGHEST,
-        preferred_element_type=jnp.float32,
-    )
-    for r in range(3):
-        pack[steps + r : steps + r + 1, :] = rows3[r].astype(jnp.float32)
-    pack[steps + 3 :, :] = jnp.zeros((pack.shape[0] - steps - 3, 128), jnp.float32)
-    for d in range(1, n_shot):
-        pack_copy(d).start()
-
-    fill_band(band_hi, 0)
-    fill_band(band_lo, 1)
+    def read_signs():
+        return [(2 * code_ref[k] - 1).astype(jnp.float32) for k in range(nsh)]
+
+    def send_pack():
+        for copy in small:
+            copy.wait()
+
+        lane = lax.broadcasted_iota(jnp.int32, (1, 128), 1)
+        lane8 = lax.broadcasted_iota(jnp.int32, (nsh, 128), 1)
+        sub8 = lax.broadcasted_iota(jnp.int32, (nsh, 128), 0)
+        rows3 = [jnp.zeros((1, 128), jnp.int32) for _ in range(3)]
+        signed = jnp.zeros((nsh, 128), jnp.float32)
+        signs = read_signs()
+        for s in range(nsh):
+            mine = lane == shot * nsh + s
+            for r, ref in enumerate((assign_ref, px_ref, py_ref)):
+                rows3[r] = jnp.where(mine, ref[s], rows3[r])
+            signed = jnp.where((lane8 == shot * nsh + s) & (sub8 == s), signs[s], signed)
+        pack[0:steps, :] = lax.dot_general(
+            wav_ref[...], signed, (((0,), (0,)), ((), ())), precision=HIGHEST,
+            preferred_element_type=jnp.float32,
+        )
+        for r in range(3):
+            pack[steps + r : steps + r + 1, :] = rows3[r].astype(jnp.float32)
+        pack[steps + 3 :, :] = jnp.zeros((pack.shape[0] - steps - 3, 128), jnp.float32)
+        for d in range(1, n_shot):
+            pack_copy(d).start()
 
     def chunk_of(i):
         return jnp.where(core == 0, nchunk - 1 - i, i)
 
-    owners = [shot_at(d) for d in range(n_shot)]
-    scales = [
-        [jnp.where(assign_ref[k] == owner, signs[k], 0.0) for k in range(nsh)]
-        for owner in owners
-    ]
-
     def encode_rows(first, count):
+        signs = read_signs()
+        scales = [
+            [jnp.where(assign_ref[k] == shot_at(d), signs[k], 0.0) for k in range(nsh)]
+            for d in range(n_shot)
+        ]
         for r in range(count):
             t = first + r
             rows = [traces[k, t] for k in range(nsh)]
@@ -372,7 +375,6 @@
     for which in range(3):
         load(which).wait()
         swap(which).wait_recv()
-    traces_in.wait()
 
     def make_sources():
         table = pack[...]
@@ -474,6 +476,12 @@
                 z_copy(new).start()
             start_x(new, chunk)
 
+        if i == 0:
+
+            @pl.when(n == 0)
+            def _():
+                send_pack()
+
         @pl.when(n == steps - 1)
         def _():
             out_away(chunk).start()
@@ -488,6 +496,7 @@
 
         @pl.when(n < encoding)
         def _():
+            pl.when(n == 0)(traces_in.wait)
             encode_rows(n * batch, batch)
 
         @pl.when(n == encoding)
@@ -552,6 +561,28 @@
         out_away(chunk).wait()
     for which in range(2):
         mis_copy(which).wait()
+
+
+def copy_kernel(a_in, b_in, a_out, b_out, a_mid, b_mid, sem_in, sem_out):
+    pieces = []
+    for src, mid, dst, count in ((a_in, a_mid, a_out, 4), (b_in, b_mid, b_out, 2)):
+        size = src.shape[1] // count
+        for i in range(count):
+            rows = pl.ds(i * size, size)
+            at = len(pieces)
+            pieces.append(
+                (
+                    pltpu.make_async_copy(src.at[0, rows], mid.at[rows], sem_in.at[at]),
+                    pltpu.make_async_copy(mid.at[rows], dst.at[0, rows], sem_out.at[at]),
+                )
+            )
+    for first, _ in pieces:
+        first.start()
+    for first, second in pieces:
+        first.wait()
+        second.start()
+    for _, second in pieces:
+        second.wait()
 
 
 def on_device(n_gx, n_shot, speed, pressure, previous, wavelets, traces, code, assign, px, py):
@@ -563,12 +594,13 @@
     hbm = pl.BlockSpec(memory_space=pltpu.HBM)
     dma = pltpu.SemaphoreType.DMA
     nchunk = half // CH
-    return pl.pallas_call(
+    shapes = (
+        jax.ShapeDtypeStruct((1, depth, wide, wide_y), f32),
+        jax.ShapeDtypeStruct((1, steps, wide, wide_y), f32),
+    )
+    results = pl.pallas_call(
         functools.partial(kernel, n_gx, n_shot),
-        out_shape=(
-            jax.ShapeDtypeStruct((1, depth, wide, wide_y), f32),
-            jax.ShapeDtypeStruct((1, steps, wide, wide_y), f32),
-        ),
+        out_shape=shapes,
         in_specs=[hbm] * 9,
         out_specs=(hbm, hbm),
         scratch_shapes=[
@@ -616,6 +648,19 @@
             collective_id=0, has_side_effects=True, vmem_limit_bytes=62 * 1024 * 1024
         ),
     )(code, assign, px, py, wavelets, speed, pressure, previous, traces)
+    return pl.pallas_call(
+        copy_kernel,
+        out_shape=shapes,
+        in_specs=[hbm] * 2,
+        out_specs=(hbm, hbm),
+        scratch_shapes=[
+            pltpu.VMEM((depth, wide, wide_y), f32),
+            pltpu.VMEM((steps, wide, wide_y), f32),
+            dma((6,)),
+            dma((6,)),
+        ],
+        compiler_params=pltpu.CompilerParams(vmem_limit_bytes=62 * 1024 * 1024),
+    )(*results)
 
 
 def solution(mesh):

time: 75.7 us -> 73 us (0.964)
  local copies, waits for them, and re-layouts: 3.46 us -> 0 us
  Pallas kernels: 71.4 us -> 72.2 us
    unnamed x2 -> x0, local copies, waits for them, and re-layouts: 3.46 us -> none
    pallas_call x1 -> x2, Pallas kernels: 71.4 us -> 72.2 us  [the longest x1 70.3 us: on_device(): pl.pallas_call(functools.partial(kernel, n_gx, n_shot), out_shape=shapes,...]
where the time goes in v4:
time: 73 us; the launch traced here: 72.8 us
  Pallas kernels  72.2 us (99%)
    pallas_call x1, Pallas kernels, on_device(): pl.pallas_call(functools.partial(kernel, n_gx, n_shot), out_shape=shapes,...  70.3 us
    pallas_call x1, Pallas kernels, on_device(): pl.pallas_call(copy_kernel, out_shape=shapes, in_specs=[hbm] * 2, out_spe...  1.91 us

profile of v4, /device:TPU:1, one launch (start us, length us, event | category | flops | bytes accessed | tf_op | source)
XLA Modules:
  0.0 72.8 jit_solution(586957517828854721)
XLA Ops:
  0.6 70.3 %shard_map.104 = (f32[1,64,16,128]{3,2,1,0:T(8,128)}, f32[1,20,16,128]{3,2,1,0:T(8,128)}) custom-call(s32[8]{0:T(128)} %code_hbm.1, s32[8]{0:T(128)} %assign_hbm.1, s32[8]{0:T(128)} %px_hbm.1, s32[8]{0:T(128)} %py_hbm.1, f32[8,20]{1,0:T(8,128)} %wav_hbm.1, f32[64,16,128]{2,1,0:T(8,128)} %speed_hbm.1, f32[1,64,16,128]{3,2,1,0:T(8,128)} %press_hbm.1, ...), custom_call_target="tpu_custom_call" | custom-call | tf_op jit(solution)/shard_map/pallas_call | solution.py:601
  70.9 1.9 %shard_map.105 = (f32[1,64,16,128]{3,2,1,0:T(8,128)}, f32[1,20,16,128]{3,2,1,0:T(8,128)}) custom-call(f32[1,64,16,128]{3,2,1,0:T(8,128)} %get-tuple-element.4.a_in, f32[1,20,16,128]{3,2,1,0:T(8,128)} %get-tuple-element.5.b_in), custom_call_target="tpu_custom_call" | custom-call | tf_op jit(solution)/shard_map/pallas_call | solution.py:651

commit v5 on v4

--- a/solution.py
+++ b/solution.py
@@ -327,8 +327,6 @@
         return [(2 * code_ref[k] - 1).astype(jnp.float32) for k in range(nsh)]
 
     def send_pack():
-        for copy in small:
-            copy.wait()
 
         lane = lax.broadcasted_iota(jnp.int32, (1, 128), 1)
         lane8 = lax.broadcasted_iota(jnp.int32, (nsh, 128), 1)
@@ -372,6 +370,17 @@
                 else:
                     obs_send[d - 1, t] = total
 
+    for copy in small:
+        copy.wait()
+    traces_in.wait()
+
+    def encode_pair(pair, carry):
+        encode_rows(2 * pair, 2)
+        return carry
+
+    lax.fori_loop(0, steps // 2, encode_pair, 0)
+    for d in range(1, n_shot):
+        obs_copy(d).start()
     for which in range(3):
         load(which).wait()
         swap(which).wait_recv()
@@ -422,7 +431,8 @@
         hi = both.astype(jnp.bfloat16)
         lo = (both - hi.astype(jnp.float32)).astype(jnp.bfloat16)
         dot = functools.partial(jnp.dot, preferred_element_type=jnp.float32)
-        along_y = dot(hi, band_hi[...]) + dot(lo, band_hi[...]) + dot(hi, band_lo[...])
+        parts = dot(jnp.concatenate([hi, lo], axis=0), band_hi[...])
+        along_y = parts[: CH * wide] + parts[CH * wide :] + dot(hi, band_lo[...])
         totals = []
         for h in range(2):
             total = along_y[:, 128 * h : 128 * (h + 1)].reshape(CH, wide, 128)
@@ -487,22 +497,9 @@
             out_away(chunk).start()
             out_copy(chunk).start()
 
-    batch = 2
-    encoding = -(-steps // batch)
-
     def one_step(n, carry):
         for i in range(nchunk):
             one_chunk(n, i)
-
-        @pl.when(n < encoding)
-        def _():
-            pl.when(n == 0)(traces_in.wait)
-            encode_rows(n * batch, batch)
-
-        @pl.when(n == encoding)
-        def _():
-            for d in range(1, n_shot):
-                obs_copy(d).start()
 
         @pl.when((n == steps - 2) & (core == 0))
         def _():

time: 73 us -> 73.3 us (level)
  no operation moved by 1% of the time
where the time goes in v5:
time: 73.3 us; the launch traced here: 73.2 us
  Pallas kernels  72.6 us (99%)
    pallas_call x1, Pallas kernels, on_device(): pl.pallas_call(functools.partial(kernel, n_gx, n_shot), out_shape=shapes,...  70.6 us
    pallas_call x1, Pallas kernels, on_device(): pl.pallas_call(copy_kernel, out_shape=shapes, in_specs=[hbm] * 2, out_spe...  1.91 us

profile of v5, /device:TPU:1, one launch (start us, length us, event | category | flops | bytes accessed | tf_op | source)
XLA Modules:
  0.0 73.2 jit_solution(15030362914462560520)
XLA Ops:
  0.6 70.6 %shard_map.104 = (f32[1,64,16,128]{3,2,1,0:T(8,128)}, f32[1,20,16,128]{3,2,1,0:T(8,128)}) custom-call(s32[8]{0:T(128)} %code_hbm.1, s32[8]{0:T(128)} %assign_hbm.1, s32[8]{0:T(128)} %px_hbm.1, s32[8]{0:T(128)} %py_hbm.1, f32[8,20]{1,0:T(8,128)} %wav_hbm.1, f32[64,16,128]{2,1,0:T(8,128)} %speed_hbm.1, f32[1,64,16,128]{3,2,1,0:T(8,128)} %press_hbm.1, ...), custom_call_target="tpu_custom_call" | custom-call | tf_op jit(solution)/shard_map/pallas_call | solution.py:598
  71.3 1.9 %shard_map.105 = (f32[1,64,16,128]{3,2,1,0:T(8,128)}, f32[1,20,16,128]{3,2,1,0:T(8,128)}) custom-call(f32[1,64,16,128]{3,2,1,0:T(8,128)} %get-tuple-element.4.a_in, f32[1,20,16,128]{3,2,1,0:T(8,128)} %get-tuple-element.5.b_in), custom_call_target="tpu_custom_call" | custom-call | tf_op jit(solution)/shard_map/pallas_call | solution.py:648
